TPU v7x, 128 devices: a whole 4x4x4 slice. The times are simulated.
128 devices in a mesh: gx: 8 (over x, core), gy: 16 (over y, z).
Axes of the slice: x: 4, y: 4, z: 4, core: 2. Of those that a mesh axis runs over, the one named last changes fastest.
Arguments:
- tracers: float32 [2, 30, 768, 1024], P(None, None, 'gy', 'gx'), may hold values from -6 to 6
- east_flow: float32 [30, 768, 1024], P(None, 'gy', 'gx'), may hold values from -0.15 to 0.15
- north_flow: float32 [30, 768, 1024], P(None, 'gy', 'gx'), may hold values from -0.15 to 0.15
- ocean_kappa: float32 [29, 768, 1024], P(None, 'gy', 'gx'), may hold values from 0.05 to 5
- land_sea: int32 [768, 1024], P('gy', 'gx'), may hold values 0 or 1
- air_temp: float32 [16, 256, 1024], P(None, 'gy', 'gx'), may hold values from -6 to 6
- air_kappa: float32 [16, 256, 1024], P(None, 'gy', 'gx'), may hold values from 0.05 to 5
- air_fluxes: float32 [4, 256, 1024], P(None, 'gy', 'gx'), may hold values from -6 to 6
- weight_tiles: float32 [128, 64, 1024], P(('gx', 'gy'))
- tile_index: int32 [128, 128, 16], P(('gx', 'gy')), may hold values from 0 to 63
- send_blocks: int32 [128, 128, 16], P(('gx', 'gy')), may hold values from 0 to 192, as said below
- receive_blocks: int32 [128, 128, 16], P(('gx', 'gy')), may hold values from 0 to 64, as said below
Outputs:
- tracers_next: float32 [2, 30, 768, 1024], P(None, None, 'gy', 'gx')
- air_temp_next: float32 [16, 256, 1024], P(None, 'gy', 'gx')
- surface_fields: float32 [4, 256, 1024], P(None, 'gy', 'gx')
Inputs may be any that keep to these rules, and one draw needn't show every extreme that they name: For each pair of devices the live slots come first along the last dimension; slot k of send_blocks[s, r] is live exactly when slot k of receive_blocks[r, s] is; 192 marks an empty slot. Every pair has at least one live slot, and some device has all 16 slots live from every device. `receive_blocks`: 64 marks an empty slot.
All inputs are finite; a program needn't handle non-finite values. No bound on the sum of `land_sea` on one device may be relied on, other than what follows from the above.
Results may differ from a plain program's by a relative error of at most 0.0003.
Values sent between devices are 32-bit elements; how exact they have to be, the bound alone decides.
A program may use at most 192 MiB of HBM per device.

v0:
```python
import jax
import jax.numpy as jnp
from jax import lax
from jax.sharding import PartitionSpec as P

NF = 4
B = 32
CAP = 16
ADV = 4
OB = 192
AB = 64


def padded(value, sides, width, wrap):
    for axis, dim in sides:
        size, length = (lax.axis_size(axis), value.shape[dim])
        up = [(i, (i + 1) % size) for i in range(size if wrap else size - 1)]
        down = [(j, i) for i, j in up]
        last = lax.slice_in_dim(value, length - width, length, axis=dim)
        leading = lax.slice_in_dim(value, 0, width, axis=dim)
        before = lax.ppermute(last, axis, up)
        after = lax.ppermute(leading, axis, down)
        value = jnp.concatenate([before, value, after], axis=dim)
    return value


def partner_2(value, axis, bit):
    return lax.ppermute(value, axis, [(i, i ^ 1 << bit) for i in range(lax.axis_size(axis))])


def transport(values, across, along, flow_east, flow_north, open_east, open_north):
    east_vel = flow_east[..., :-1]
    face_east = (
        open_east[:, :-1]
        * open_east[:, 1:]
        * (
            jnp.maximum(east_vel, 0.0) * across[..., :-1]
            + jnp.minimum(east_vel, 0.0) * across[..., 1:]
        )
    )
    north_vel = flow_north[..., :-1, :]
    face_north = (
        open_north[:-1, :]
        * open_north[1:, :]
        * (
            jnp.maximum(north_vel, 0.0) * along[..., :-1, :]
            + jnp.minimum(north_vel, 0.0) * along[..., 1:, :]
        )
    )
    return (
        values
        - (face_east[..., 1:] - face_east[..., :-1])
        - (face_north[..., 1:, :] - face_north[..., :-1, :])
    )


def thomas(below_coef, diag_coef, above_coef, source_terms):
    ratio_list = [above_coef[0] / diag_coef[0]]
    value_list = [source_terms[0] / diag_coef[0]]
    for layer_index in range(1, len(diag_coef)):
        pivot_value = diag_coef[layer_index] - below_coef[layer_index] * ratio_list[-1]
        ratio_list.append(above_coef[layer_index] / pivot_value)
        value_list.append(
            (source_terms[layer_index] - below_coef[layer_index] * value_list[-1]) / pivot_value
        )
    result = [value_list[-1]]
    for layer_index in range(len(diag_coef) - 2, -1, -1):
        result.append(value_list[layer_index] - ratio_list[layer_index] * result[-1])
    return result[::-1]


def ocean_mix(advected, ocean_kappa, sea, forcing):
    layers = advected.shape[1]
    links = [ocean_kappa[layer_index] * sea for layer_index in range(layers - 1)]
    flat_zero = jnp.zeros_like(sea)
    below_coef = [flat_zero] + [-link_value for link_value in links]
    above_coef = [-link_value for link_value in links] + [flat_zero]
    diag_coef = [
        1.0 - below_coef[layer_index] - above_coef[layer_index] for layer_index in range(layers)
    ]
    sources = [advected[:, layer_index] for layer_index in range(layers)]
    sources[0] = sources[0] + forcing
    return jnp.stack(thomas(below_coef, diag_coef, above_coef, sources), axis=1)


def air_mix(air_temp, air_kappa, ground):
    layers = air_temp.shape[0]
    flat_zero = jnp.zeros_like(ground)
    below_coef = [flat_zero] + [-air_kappa[layer_index] for layer_index in range(1, layers)]
    above_coef = [-air_kappa[layer_index + 1] for layer_index in range(layers - 1)] + [flat_zero]
    diag_coef = [1.0 + air_kappa[0] - above_coef[0]] + [
        1.0 - below_coef[layer_index] - above_coef[layer_index] for layer_index in range(1, layers)
    ]
    sources = [air_temp[0] + air_kappa[0] * ground] + [
        air_temp[layer_index] for layer_index in range(1, layers)
    ]
    return jnp.stack(thomas(below_coef, diag_coef, above_coef, sources), axis=0)


def lon_rim(values):
    return padded(values, (("gx", 2),), 1, True)


def lat_rim(values):
    return padded(values, (("gy", 1),), 1, False)


def fold_row(top_row):
    partner = top_row
    for bit_number in range(lax.axis_size("gx").bit_length() - 1):
        partner = partner_2(partner, "gx", bit_number)
    return jnp.flip(partner, 1)


def local_blocks(fields):
    field_count, rows_here, cols_here = fields.shape
    shaped = fields.reshape(field_count, rows_here, cols_here // B, B).transpose(1, 2, 0, 3)
    return shaped.reshape(rows_here * (cols_here // B), field_count * B)


def local_fields(blocks, rows_here, cols_here):
    shaped = blocks.reshape(rows_here, cols_here // B, NF, B).transpose(2, 0, 1, 3)
    return shaped.reshape(NF, rows_here, cols_here)


def inbound(buffer):
    return lax.all_to_all(buffer, ("gx", "gy"), split_axis=0, concat_axis=0, tiled=True)


def outbound(buffer):
    return lax.all_to_all(buffer, ("gx", "gy"), split_axis=0, concat_axis=0, tiled=True)


def shards(
    tracers,
    east_flow,
    north_flow,
    ocean_kappa,
    land_sea,
    air_temp,
    air_kappa,
    air_fluxes,
    weight_tiles,
    tile_index,
    send_blocks,
    receive_blocks,
):
    device_count = lax.axis_size("gx") * lax.axis_size("gy")
    slot_count = device_count * CAP
    sea = land_sea.astype(jnp.float32)
    rows_here, cols_here = sea.shape
    air_rows, air_cols = (air_temp.shape[1], air_temp.shape[2])
    at_top = lax.axis_index("gy") == lax.axis_size("gy") - 1
    tiles = jnp.take(weight_tiles[0], tile_index[0].reshape(slot_count), axis=0).reshape(
        slot_count, B, B
    )
    chosen = send_blocks[0].reshape(slot_count)
    targets = receive_blocks[0].reshape(slot_count)
    air_local = local_blocks(air_fluxes)
    picked = jnp.take(air_local, jnp.minimum(targets, AB - 1), axis=0)
    picked = jnp.where((targets < AB)[:, None], picked, 0.0)
    arrived = inbound(picked.reshape(device_count, CAP, NF * B)).reshape(slot_count, NF, B)
    spread = jnp.einsum("sab,sfa->sfb", tiles, arrived, precision=lax.Precision.HIGHEST).reshape(
        slot_count, NF * B
    )
    owner_map = (jnp.arange(OB, dtype=jnp.int32)[:, None] == chosen[None, :]).astype(jnp.float32)
    forcing_fields = local_fields(
        jnp.dot(owner_map, spread, precision=lax.Precision.HIGHEST), rows_here, cols_here
    )
    layers = east_flow.shape[0]
    tracer_count = tracers.shape[0]
    stack_count = tracer_count * layers
    east_stack = lon_rim(jnp.concatenate([east_flow, sea[None]], axis=0))
    north_stack = lat_rim(jnp.concatenate([north_flow, sea[None]], axis=0))
    flow_east, open_east = (east_stack[:layers], east_stack[layers])
    flow_north, open_north = (north_stack[:layers], north_stack[layers])
    folded_sea = fold_row(sea[-1:, :])[0]
    open_north = open_north.at[-1].set(jnp.where(at_top, folded_sea, open_north[-1]))
    values = tracers
    for step_index in range(ADV):
        flat = values.reshape(stack_count, rows_here, cols_here)
        across = lon_rim(flat).reshape(tracer_count, layers, rows_here, cols_here + 2)
        along = lat_rim(flat)
        reflected = fold_row(flat[:, -1, :])
        along = along.at[:, -1, :].set(jnp.where(at_top, reflected, along[:, -1, :]))
        along = along.reshape(tracer_count, layers, rows_here + 2, cols_here)
        values = transport(values, across, along, flow_east, flow_north, open_east, open_north)
    forcing = jnp.stack([sea * forcing_fields[0], sea * forcing_fields[1]], axis=0)
    tracers_next = ocean_mix(values, ocean_kappa, sea, forcing)
    surface = jnp.stack(
        [
            sea * tracers_next[0, 0],
            sea,
            sea * (east_flow[0] + 0.1 * jnp.tanh(forcing_fields[2])),
            sea * (north_flow[0] + 0.1 * jnp.tanh(forcing_fields[3])),
        ],
        axis=0,
    )
    ocean_local = local_blocks(surface)
    lifted = jnp.take(ocean_local, jnp.minimum(chosen, OB - 1), axis=0).reshape(slot_count, NF, B)
    mapped = jnp.einsum("sab,sfb->sfa", tiles, lifted, precision=lax.Precision.HIGHEST)
    mapped = jnp.where((chosen < OB)[:, None, None], mapped, 0.0).reshape(device_count, CAP, NF * B)
    received = outbound(mapped).reshape(slot_count, NF * B)
    target_map = (jnp.arange(AB, dtype=jnp.int32)[:, None] == targets[None, :]).astype(jnp.float32)
    surface_fields = local_fields(
        jnp.dot(target_map, received, precision=lax.Precision.HIGHEST), air_rows, air_cols
    )
    ground = air_temp[0] * (1.0 - surface_fields[1]) + surface_fields[0]
    air_temp_next = air_mix(air_temp, air_kappa, ground)
    return (tracers_next, air_temp_next, surface_fields)


def solution(mesh):
    return jax.shard_map(
        shards,
        mesh=mesh,
        in_specs=(
            P(None, None, "gy", "gx"),
            P(None, "gy", "gx"),
            P(None, "gy", "gx"),
            P(None, "gy", "gx"),
            P("gy", "gx"),
            P(None, "gy", "gx"),
            P(None, "gy", "gx"),
            P(None, "gy", "gx"),
            P(("gx", "gy"), None, None),
            P(("gx", "gy"), None, None),
            P(("gx", "gy"), None, None),
            P(("gx", "gy"), None, None),
        ),
        out_specs=(P(None, None, "gy", "gx"), P(None, "gy", "gx"), P(None, "gy", "gx")),
        check_vma=False,
    )
```

profile of v0, /device:TPU:1, one launch (start us, length us, event | category | flops | bytes accessed | tf_op | source)
XLA Modules:
  0.0 417.5 jit_solution(18224606905593192547)
XLA Ops:
  5.2 4.3 %collective-permute-start.4 = (f32[31,1,128]{2,1,0:T(1,128)S(1)}, f32[31,1,128]{2,1,0:T(1,128)S(1)}, u32[]{:S(2)}, u32[]{:S(2)}) collective-permute-start(f32[31,1,128]{2,1,0:T(1,128)S(1)} %get-tuple-element.215), channel_id=1, source_target_pairs={{0,1},{1,2},{2,3},{3,4},{4,5},{5,6},{6,7},{7,8},{8,9},{9,10},{10,1... | collective-permute-start | bytes 47624 | tf_op jit(solution)/shard_map/ppermute | solution.py:21
  13.2 5.5 %gather_fusion = f32[2048,128]{1,0:T(8,128)S(1)} fusion(f32[64,128]{1,0:T(8,128)S(1)} %reshape.688, s32[2048]{0:T(1024)S(1)} %broadcast_clamp_fusion.2), kind=kCustom, calls=%fused_computation | custom fusion | bytes 2105344 | tf_op jit(solution)/shard_map/jit(_take)/gather | solution.py:160
  18.6 2.2 select_select_fusion
  20.8 13.0 %all-to-all-start = ((f32[128,16,128]{2,1,0:T(8,128)}), f32[128,16,128]{2,1,0:T(8,128)}, u32[]{:S(2)}, u32[]{:S(2)}) async-start(f32[128,16,128]{2,1,0:T(8,128)} %select_select_fusion), calls=%async_computation | async-start | bytes 2097152 | tf_op jit(solution)/shard_map/all_to_all | solution.py:127
  34.4 1.7 collective-permute-start
  37.5 9.8 %gather_fusion.1 = f32[2048,1024]{1,0:T(8,128)} fusion(f32[64,1024]{1,0:T(8,128)S(1)} %bitcast.474, s32[2048]{0:T(1024)S(1)} %get-tuple-element.273), kind=kCustom, calls=%fused_computation.1 | custom fusion | bytes 16785408 | tf_op jit(solution)/shard_map/jit(_take)/gather | solution.py:154
  47.3 9.2 %copy.223 = f32[2048,1024]{0,1:T(8,128)} copy(f32[2048,1024]{1,0:T(8,128)} %gather_fusion.1) | data formatting | bytes 16777216 | tf_op jit(solution)/shard_map/jit(_take)/gather | solution.py:154
  56.5 8.5 %broadcast_select_fusion = f32[2048,32,32]{0,2,1:T(8,128)} fusion(f32[2048,32,32]{0,2,1:T(8,128)} %bitcast.487, pred[2048]{0:T(1024)(128)(4,1)S(1)} %compare_and_fusion.1), kind=kLoop, calls=%fused_computation.3 | loop fusion | flops 2097152 | bytes 16779264 | tf_op jit(solution)/shard_map/jit(_take)/select_n | solution.py:154
  69.0 2.4 collective-permute-start.8
  71.5 2.0 copy.179
  75.5 3.1 collective-permute-start.2
  81.5 3.0 fusion.31
  84.5 4.3 %collective-permute-start.9 = (f32[60,1,128]{2,0,1:T(8,128)S(1)}, f32[60,1,128]{2,0,1:T(8,128)S(1)}, u32[]{:S(2)}, u32[]{:S(2)}) collective-permute-start(f32[60,1,128]{2,0,1:T(8,128)S(1)} %copy.273), channel_id=1, source_target_pairs={{0,1},{1,2},{2,3},{3,4},{4,5},{5,6},{6,7},{7,8},{8,9},{9,10},{10,1... | collective-permute-start | bytes 92168 | tf_op jit(solution)/shard_map/ppermute | solution.py:21
  88.8 1.7 copy.181
  90.6 3.2 collective-permute-start.11
  93.9 1.7 copy.178
  95.6 4.8 %fusion.1 = f32[2,30,48,129]{3,2,1,0:T(8,128)} fusion(f32[2,30,48,128]{3,2,1,0:T(8,128)S(1)} %copy-done.2, f32[2,30,48,1]{3,2,1,0:T(8,128)} %copy.178, f32[2,30,48,1]{3,2,1,0:T(8,128)} %copy.181, f32[30,48,129]{2,1,0:T(8,128)} %get-tuple-element.193, f32[30,48,129]{2,1,0:T(8,128)S(1)} %get-tuple-element.192, f32[48,129]{1,0:T(8,128)S(1)} %slice_multiply_fusion.8), kind=kLoop, calls=%fused_computation.6 | loop fusion | flops 2229120 | bytes 4494528 | tf_op jit(solution)/shard_map/mul | solution.py:34
  100.6 2.2 fusion.36
  103.3 12.5 %collective-permute-start.13 = (f32[60,128]{1,0:T(8,128)S(1)}, f32[60,128]{1,0:T(8,128)S(1)}, u32[]{:S(2)}, u32[]{:S(2)}) collective-permute-start(f32[60,128]{1,0:T(8,128)S(1)} %collective-permute-done.12), channel_id=1, source_target_pairs={{0,64},{16,80},{32,96},{48,112},{64,0},{80,16},{96,32},{112,48},{1... | collective-permute-start | bytes 92168 | tf_op jit(solution)/shard_map/ppermute | solution.py:28
  117.3 2.4 collective-permute-done.13
  119.8 1.7 scatter.19
  121.5 2.7 fusion.15
  125.3 1.6 fusion.234
  126.9 2.3 collective-permute-start.18
  129.2 1.9 copy.249
  132.7 2.6 collective-permute-start.16
  136.7 1.7 copy.189
  138.5 1.7 copy.187
  140.6 4.7 %fusion.3 = f32[2,30,48,129]{3,2,1,0:T(8,128)} fusion(f32[2,30,48,128]{3,2,1,0:T(8,128)S(1)} %fusion.25, f32[2,30,48,1]{3,2,1,0:T(8,128)} %copy.187, f32[2,30,48,1]{3,2,1,0:T(8,128)} %copy.189, f32[30,48,129]{2,1,0:T(8,128)} %get-tuple-element.193, f32[30,48,129]{2,1,0:T(8,128)S(1)} %copy-done.4, f32[48,129]{1,0:T(8,128)S(1)} %slice_multiply_fusion.8), kind=kLoop, calls=%fused_computation.10 | loop fusion | flops 2229120 | bytes 4494528 | tf_op jit(solution)/shard_map/mul | solution.py:34
  145.4 2.8 collective-permute-start.20
  149.9 1.7 scatter.20
  151.7 2.5 fusion.13
  155.2 1.6 fusion.232
  156.8 3.4 collective-permute-start.25
  160.2 1.9 copy.253
  162.7 1.6 collective-permute-start.21
  164.4 4.3 %collective-permute-start.23 = (f32[60,1,128]{2,0,1:T(8,128)S(1)}, f32[60,1,128]{2,0,1:T(8,128)S(1)}, u32[]{:S(2)}, u32[]{:S(2)}) collective-permute-start(f32[60,1,128]{2,0,1:T(8,128)S(1)} %copy.271), channel_id=1, source_target_pairs={{0,1},{1,2},{2,3},{3,4},{4,5},{5,6},{6,7},{7,8},{8,9},{9,10},{10,1... | collective-permute-start | bytes 92168 | tf_op jit(solution)/shard_map/ppermute | solution.py:21
  170.0 1.7 copy.199
  171.8 1.7 copy.197
  174.1 4.7 %fusion.5 = f32[2,30,48,129]{3,2,1,0:T(8,128)} fusion(f32[2,30,48,128]{3,2,1,0:T(8,128)S(1)} %fusion.23, f32[2,30,48,1]{3,2,1,0:T(8,128)} %copy.197, f32[2,30,48,1]{3,2,1,0:T(8,128)} %copy.199, f32[30,48,129]{2,1,0:T(8,128)} %get-tuple-element.193, f32[30,48,129]{2,1,0:T(8,128)S(1)} %copy-done.5, f32[48,129]{1,0:T(8,128)S(1)} %slice_multiply_fusion.8), kind=kLoop, calls=%fused_computation.14 | loop fusion | flops 2229120 | bytes 4494528 | tf_op jit(solution)/shard_map/mul | solution.py:34
  178.9 1.6 collective-permute-start.27
  183.4 1.7 scatter.21
  185.1 2.7 fusion.11
  188.9 1.6 fusion.230
  190.5 2.9 collective-permute-start.32
  193.5 2.0 copy.257
  199.0 26.3 %copy.224 = f32[2048,32,32]{2,1,0:T(8,128)} copy(f32[2048,32,32]{0,2,1:T(8,128)} %broadcast_select_fusion) | data formatting | bytes 16777216 | tf_op jit(solution)/shard_map/jit(_take)/select_n | solution.py:154
  225.4 5.5 %collective-permute-start.30 = (f32[60,1,128]{2,0,1:T(8,128)S(1)}, f32[60,1,128]{2,0,1:T(8,128)S(1)}, u32[]{:S(2)}, u32[]{:S(2)}) collective-permute-start(f32[60,1,128]{2,0,1:T(8,128)S(1)} %copy.270), channel_id=1, source_target_pairs={{0,1},{1,2},{2,3},{3,4},{4,5},{5,6},{6,7},{7,8},{8,9},{9,10},{10,1... | collective-permute-start | bytes 92168 | tf_op jit(solution)/shard_map/ppermute | solution.py:21
  232.3 1.7 copy.210
  234.1 1.7 copy.207
  236.4 4.7 %fusion.7 = f32[2,30,48,129]{3,2,1,0:T(8,128)} fusion(f32[2,30,48,128]{3,2,1,0:T(8,128)S(1)} %fusion.21, f32[2,30,48,1]{3,2,1,0:T(8,128)} %copy.207, f32[2,30,48,1]{3,2,1,0:T(8,128)} %copy.210, f32[30,48,129]{2,1,0:T(8,128)} %get-tuple-element.193, f32[30,48,129]{2,1,0:T(8,128)S(1)} %copy-done.6, f32[48,129]{1,0:T(8,128)S(1)} %slice_multiply_fusion.8), kind=kLoop, calls=%fused_computation.18 | loop fusion | flops 2229120 | bytes 4494528 | tf_op jit(solution)/shard_map/mul | solution.py:34
  241.2 2.4 collective-permute-start.34
  245.7 1.8 scatter.24
  247.5 2.5 fusion.9
  250.9 4.7 %reshape.689 = f32[2048,4,32]{2,1,0:T(4,128)} reshape(f32[128,16,128]{2,1,0:T(8,128)} %all-to-all-done) | data formatting | bytes 2097152 | tf_op jit(solution)/shard_map/reshape | solution.py:162
  255.7 31.2 %fusion.239 = f32[2048,4,32]{2,1,0:T(4,128)} fusion(f32[2048,4,32]{2,1,0:T(4,128)} %reshape.689, f32[2048,32,32]{2,1,0:T(8,128)} %copy.224), kind=kOutput, calls=%fused_computation.523 | convolution fusion | flops 100663296 | bytes 10485760 | tf_op jit(solution)/shard_map/sab,sfa->sfb/dot_general | solution.py:163
  286.9 3.5 copy.225
  303.3 5.5 %gather_fusion.2 = f32[2048,128]{1,0:T(8,128)S(1)} fusion(f32[192,128]{1,0:T(8,128)S(1)} %reshape.691, s32[2048]{0:T(1024)S(1)} %copy-done.75), kind=kCustom, calls=%fused_computation.2 | custom fusion | bytes 2105344 | tf_op jit(solution)/shard_map/jit(_take)/gather | solution.py:200
  310.0 2.3 constant_dynamic-update-slice_fusion.29
  314.0 3.1 copy.238
  317.1 57.0 %broadcast_select_fusion.1 = f32[2048,4,32]{2,1,0:T(4,128)} fusion(pred[2048]{0:T(1024)(128)(4,1)S(1)} %copy-done.72, f32[2048,4,32]{2,1,0:T(4,128)} %copy.238, f32[2048,32,32]{2,1,0:T(8,128)} %copy.224), kind=kOutput, calls=%fused_computation.20 | convolution fusion | flops 100925440 | bytes 10487808 | tf_op jit(solution)/shard_map/sab,sfb->sfa/dot_general | solution.py:201
  374.1 4.5 %reshape.692 = f32[128,16,128]{2,1,0:T(8,128)} reshape(f32[2048,4,32]{2,1,0:T(4,128)} %broadcast_select_fusion.1) | data formatting | bytes 2097152 | tf_op jit(solution)/shard_map/reshape | solution.py:202
  378.6 15.8 %all-to-all-start.1 = ((f32[128,16,128]{2,1,0:T(8,128)}), f32[128,16,128]{2,1,0:T(8,128)S(1)}, u32[]{:S(2)}, u32[]{:S(2)}) async-start(f32[128,16,128]{2,1,0:T(8,128)} %reshape.692), calls=%async_computation.1 | async-start | bytes 2097152 | tf_op jit(solution)/shard_map/all_to_all | solution.py:131
  398.2 15.1 %all-to-all-done.1 = f32[128,16,128]{2,1,0:T(8,128)S(1)} async-done(((f32[128,16,128]{2,1,0:T(8,128)}), f32[128,16,128]{2,1,0:T(8,128)S(1)}, u32[]{:S(2)}, u32[]{:S(2)}) %all-to-all-start.1) | async-done | bytes 1048608 | tf_op jit(solution)/shard_map/all_to_all | solution.py:131
  (389 shorter events, 66.8 us)
Async XLA Ops:
  0.6 36.9 %copy-start = (f32[1,64,1024]{2,1,0:T(8,128)S(1)}, f32[1,64,1024]{2,1,0:T(8,128)}, u32[]{:S(2)}) copy-start(f32[1,64,1024]{2,1,0:T(8,128)} %param.30) | copy-start | bytes 786436
  1.4 65.2 %collective-permute-start.6 = (f32[1,128]{1,0:T(1,128)S(1)}, f32[1,128]{1,0:T(1,128)S(1)}, u32[]{:S(2)}, u32[]{:S(2)}) collective-permute-start(f32[1,128]{1,0:T(1,128)S(1)} %slice.798), channel_id=1, source_target_pairs={{0,16},{16,0},{32,48},{48,32},{64,80},{80,64},{96,112},{112,96},{1... | collective-permute-start | bytes 1544 | tf_op jit(solution)/shard_map/ppermute | solution.py:28
  3.9 96.4 %collective-permute-start.5 = (f32[31,1,128]{2,1,0:T(1,128)S(1)}, f32[31,1,128]{2,1,0:T(1,128)S(1)}, u32[]{:S(2)}, u32[]{:S(2)}) collective-permute-start(f32[31,1,128]{2,1,0:T(1,128)S(1)} %get-tuple-element.214), channel_id=1, source_target_pairs={{1,0},{2,1},{3,2},{4,3},{5,4},{6,5},{7,6},{8,7},{9,8},{10,9},{11,1... | collective-permute-start | bytes 47624 | tf_op jit(solution)/shard_map/ppermute | solution.py:22
  5.2 95.2 %collective-permute-start.4 = (f32[31,1,128]{2,1,0:T(1,128)S(1)}, f32[31,1,128]{2,1,0:T(1,128)S(1)}, u32[]{:S(2)}, u32[]{:S(2)}) collective-permute-start(f32[31,1,128]{2,1,0:T(1,128)S(1)} %get-tuple-element.215), channel_id=1, source_target_pairs={{0,1},{1,2},{2,3},{3,4},{4,5},{5,6},{6,7},{7,8},{8,9},{9,10},{10,1... | collective-permute-start | bytes 47624 | tf_op jit(solution)/shard_map/ppermute | solution.py:21
  20.8 13.0 %copy-start.19 = (f32[30,48,128]{2,1,0:T(8,128)S(1)}, f32[30,48,128]{2,1,0:T(8,128)}, u32[]{:S(2)}) copy-start(f32[30,48,128]{2,1,0:T(8,128)} %param.23) | copy-start | bytes 2211844
  20.8 230.1 %all-to-all-start = ((f32[128,16,128]{2,1,0:T(8,128)}), f32[128,16,128]{2,1,0:T(8,128)}, u32[]{:S(2)}, u32[]{:S(2)}) async-start(f32[128,16,128]{2,1,0:T(8,128)} %select_select_fusion), calls=%async_computation | async-start | bytes 2097152 | tf_op jit(solution)/shard_map/all_to_all | solution.py:127
  34.4 41.2 %collective-permute-start = (f32[31,48,1]{1,0,2:T(8,128)S(1)}, f32[31,48,1]{1,0,2:T(8,128)S(1)}, u32[]{:S(2)}, u32[]{:S(2)}) collective-permute-start(f32[31,48,1]{1,0,2:T(8,128)S(1)} %copy.171), channel_id=1, source_target_pairs={{0,16},{16,32},{32,48},{48,64},{64,80},{80,96},{96,112},{112,0},{1... | collective-permute-start | bytes 17864 | tf_op jit(solution)/shard_map/ppermute | solution.py:21
  36.3 42.7 %collective-permute-start.1 = (f32[31,48,1]{1,0,2:T(8,128)S(1)}, f32[31,48,1]{1,0,2:T(8,128)S(1)}, u32[]{:S(2)}, u32[]{:S(2)}) collective-permute-start(f32[31,48,1]{1,0,2:T(8,128)S(1)} %copy.172), channel_id=1, source_target_pairs={{16,0},{32,16},{48,32},{64,48},{80,64},{96,80},{112,96},{0,112},{1... | collective-permute-start | bytes 17864 | tf_op jit(solution)/shard_map/ppermute | solution.py:22
  56.5 8.5 %copy-start.2 = (f32[2,30,48,128]{3,2,1,0:T(8,128)S(1)}, f32[2,30,48,128]{3,2,1,0:T(8,128)}, u32[]{:S(2)}) copy-start(f32[2,30,48,128]{3,2,1,0:T(8,128)} %param.22) | copy-start | bytes 4423684
  66.6 2.4 collective-permute-start.7
  69.0 5.2 %collective-permute-start.8 = (f32[1,128]{1,0:T(1,128)S(1)}, f32[1,128]{1,0:T(1,128)S(1)}, u32[]{:S(2)}, u32[]{:S(2)}) collective-permute-start(f32[1,128]{1,0:T(1,128)S(1)} %collective-permute-done.7), channel_id=1, source_target_pairs={{0,64},{16,80},{32,96},{48,112},{64,0},{80,16},{96,32},{112,48},{1... | collective-permute-start | bytes 1544 | tf_op jit(solution)/shard_map/ppermute | solution.py:28
  74.2 28.6 %collective-permute-start.10 = (f32[60,1,128]{2,0,1:T(8,128)S(1)}, f32[60,1,128]{2,0,1:T(8,128)S(1)}, u32[]{:S(2)}, u32[]{:S(2)}) collective-permute-start(f32[60,1,128]{2,0,1:T(8,128)S(1)} %copy.247), channel_id=1, source_target_pairs={{1,0},{2,1},{3,2},{4,3},{5,4},{6,5},{7,6},{8,7},{9,8},{10,9},{11,1... | collective-permute-start | bytes 92168 | tf_op jit(solution)/shard_map/ppermute | solution.py:22
  75.5 15.0 %collective-permute-start.2 = (f32[60,48,1]{0,1,2:T(8,128)S(1)}, f32[60,48,1]{0,1,2:T(8,128)S(1)}, u32[]{:S(2)}, u32[]{:S(2)}) collective-permute-start(f32[60,48,1]{0,1,2:T(8,128)S(1)} %copy.176), channel_id=1, source_target_pairs={{0,16},{16,32},{32,48},{48,64},{64,80},{80,96},{96,112},{112,0},{1... | collective-permute-start | bytes 34568 | tf_op jit(solution)/shard_map/ppermute | solution.py:21
  79.0 5.5 %collective-permute-start.3 = (f32[60,48,1]{0,1,2:T(8,128)S(1)}, f32[60,48,1]{0,1,2:T(8,128)S(1)}, u32[]{:S(2)}, u32[]{:S(2)}) collective-permute-start(f32[60,48,1]{0,1,2:T(8,128)S(1)} %copy.179), channel_id=1, source_target_pairs={{16,0},{32,16},{48,32},{64,48},{80,64},{96,80},{112,96},{0,112},{1... | collective-permute-start | bytes 34568 | tf_op jit(solution)/shard_map/ppermute | solution.py:22
  84.5 11.1 %copy-start.3 = (f32[30,48,129]{2,1,0:T(8,128)}, f32[30,48,129]{2,1,0:T(8,128)S(1)}, u32[]{:S(2)}) copy-start(f32[30,48,129]{2,1,0:T(8,128)S(1)} %get-tuple-element.192) | copy-start | bytes 2229124
  84.5 18.3 %collective-permute-start.9 = (f32[60,1,128]{2,0,1:T(8,128)S(1)}, f32[60,1,128]{2,0,1:T(8,128)S(1)}, u32[]{:S(2)}, u32[]{:S(2)}) collective-permute-start(f32[60,1,128]{2,0,1:T(8,128)S(1)} %copy.273), channel_id=1, source_target_pairs={{0,1},{1,2},{2,3},{3,4},{4,5},{5,6},{6,7},{7,8},{8,9},{9,10},{10,1... | collective-permute-start | bytes 92168 | tf_op jit(solution)/shard_map/ppermute | solution.py:21
  90.6 9.9 %collective-permute-start.11 = (f32[60,128]{1,0:T(8,128)S(1)}, f32[60,128]{1,0:T(8,128)S(1)}, u32[]{:S(2)}, u32[]{:S(2)}) collective-permute-start(f32[60,128]{1,0:T(8,128)S(1)} %bitcast.510), channel_id=1, source_target_pairs={{0,16},{16,0},{32,48},{48,32},{64,80},{80,64},{96,112},{112,96},{1... | collective-permute-start | bytes 92168 | tf_op jit(solution)/shard_map/ppermute | solution.py:28
  100.5 2.8 collective-permute-start.12
  102.8 18.8 %copy-start.7 = (f32[30,49,128]{2,1,0:T(8,128)}, f32[30,49,128]{2,1,0:T(8,128)S(1)}, u32[]{:S(2)}) copy-start(f32[30,49,128]{2,1,0:T(8,128)S(1)} %get-tuple-element.210) | copy-start | bytes 2257924
  103.3 16.3 %collective-permute-start.13 = (f32[60,128]{1,0:T(8,128)S(1)}, f32[60,128]{1,0:T(8,128)S(1)}, u32[]{:S(2)}, u32[]{:S(2)}) collective-permute-start(f32[60,128]{1,0:T(8,128)S(1)} %collective-permute-done.12), channel_id=1, source_target_pairs={{0,64},{16,80},{32,96},{48,112},{64,0},{80,16},{96,32},{112,48},{1... | collective-permute-start | bytes 92168 | tf_op jit(solution)/shard_map/ppermute | solution.py:28
  126.9 13.3 %collective-permute-start.18 = (f32[60,128]{1,0:T(8,128)S(1)}, f32[60,128]{1,0:T(8,128)S(1)}, u32[]{:S(2)}, u32[]{:S(2)}) collective-permute-start(f32[60,128]{1,0:T(8,128)S(1)} %bitcast.512), channel_id=1, source_target_pairs={{0,16},{16,0},{32,48},{48,32},{64,80},{80,64},{96,112},{112,96},{1... | collective-permute-start | bytes 92168 | tf_op jit(solution)/shard_map/ppermute | solution.py:28
  131.6 6.8 %collective-permute-start.14 = (f32[60,48,1]{1,2,0:T(1,128)S(1)}, f32[60,48,1]{1,2,0:T(1,128)S(1)}, u32[]{:S(2)}, u32[]{:S(2)}) collective-permute-start(f32[60,48,1]{1,2,0:T(1,128)S(1)} %copy.248), channel_id=1, source_target_pairs={{0,16},{16,32},{32,48},{48,64},{64,80},{80,96},{96,112},{112,0},{1... | collective-permute-start | bytes 34568 | tf_op jit(solution)/shard_map/ppermute | solution.py:21
  132.0 4.7 %collective-permute-start.15 = (f32[60,48,1]{1,2,0:T(1,128)S(1)}, f32[60,48,1]{1,2,0:T(1,128)S(1)}, u32[]{:S(2)}, u32[]{:S(2)}) collective-permute-start(f32[60,48,1]{1,2,0:T(1,128)S(1)} %copy.249), channel_id=1, source_target_pairs={{16,0},{32,16},{48,32},{64,48},{80,64},{96,80},{112,96},{0,112},{1... | collective-permute-start | bytes 34568 | tf_op jit(solution)/shard_map/ppermute | solution.py:22
  132.7 12.6 %collective-permute-start.16 = (f32[60,1,128]{2,0,1:T(8,128)S(1)}, f32[60,1,128]{2,0,1:T(8,128)S(1)}, u32[]{:S(2)}, u32[]{:S(2)}) collective-permute-start(f32[60,1,128]{2,0,1:T(8,128)S(1)} %copy.272), channel_id=1, source_target_pairs={{0,1},{1,2},{2,3},{3,4},{4,5},{5,6},{6,7},{7,8},{8,9},{9,10},{10,1... | collective-permute-start | bytes 92168 | tf_op jit(solution)/shard_map/ppermute | solution.py:21
  135.4 9.9 %collective-permute-start.17 = (f32[60,1,128]{2,0,1:T(8,128)S(1)}, f32[60,1,128]{2,0,1:T(8,128)S(1)}, u32[]{:S(2)}, u32[]{:S(2)}) collective-permute-start(f32[60,1,128]{2,0,1:T(8,128)S(1)} %copy.251), channel_id=1, source_target_pairs={{1,0},{2,1},{3,2},{4,3},{5,4},{6,5},{7,6},{8,7},{9,8},{10,9},{11,1... | collective-permute-start | bytes 92168 | tf_op jit(solution)/shard_map/ppermute | solution.py:22
  140.1 5.3 %collective-permute-start.19 = (f32[60,128]{1,0:T(8,128)S(1)}, f32[60,128]{1,0:T(8,128)S(1)}, u32[]{:S(2)}, u32[]{:S(2)}) collective-permute-start(f32[60,128]{1,0:T(8,128)S(1)} %collective-permute-done.18), channel_id=1, source_target_pairs={{0,32},{16,48},{32,0},{48,16},{64,96},{80,112},{96,64},{112,80},{1... | collective-permute-start | bytes 92168 | tf_op jit(solution)/shard_map/ppermute | solution.py:28
  145.4 6.2 %copy-start.8 = (f32[30,49,128]{2,1,0:T(8,128)S(1)}, f32[30,49,128]{2,1,0:T(8,128)}, u32[]{:S(2)}) copy-start(f32[30,49,128]{2,1,0:T(8,128)} %copy-done.7) | copy-start | bytes 2257924
  145.4 6.2 %copy-start.11 = (f32[30,49,128]{2,1,0:T(8,128)S(1)}, f32[30,49,128]{2,1,0:T(8,128)}, u32[]{:S(2)}) copy-start(f32[30,49,128]{2,1,0:T(8,128)} %get-tuple-element.211) | copy-start | bytes 2257924
  145.4 4.3 %collective-permute-start.20 = (f32[60,128]{1,0:T(8,128)S(1)}, f32[60,128]{1,0:T(8,128)S(1)}, u32[]{:S(2)}, u32[]{:S(2)}) collective-permute-start(f32[60,128]{1,0:T(8,128)S(1)} %collective-permute-done.19), channel_id=1, source_target_pairs={{0,64},{16,80},{32,96},{48,112},{64,0},{80,16},{96,32},{112,48},{1... | collective-permute-start | bytes 92168 | tf_op jit(solution)/shard_map/ppermute | solution.py:28
  156.8 16.7 %collective-permute-start.25 = (f32[60,128]{1,0:T(8,128)S(1)}, f32[60,128]{1,0:T(8,128)S(1)}, u32[]{:S(2)}, u32[]{:S(2)}) collective-permute-start(f32[60,128]{1,0:T(8,128)S(1)} %bitcast.513), channel_id=1, source_target_pairs={{0,16},{16,0},{32,48},{48,32},{64,80},{80,64},{96,112},{112,96},{1... | collective-permute-start | bytes 92168 | tf_op jit(solution)/shard_map/ppermute | solution.py:28
  162.7 9.0 %collective-permute-start.21 = (f32[60,48,1]{0,1,2:T(8,128)S(1)}, f32[60,48,1]{0,1,2:T(8,128)S(1)}, u32[]{:S(2)}, u32[]{:S(2)}) collective-permute-start(f32[60,48,1]{0,1,2:T(8,128)S(1)} %copy.252), channel_id=1, source_target_pairs={{0,16},{16,32},{32,48},{48,64},{64,80},{80,96},{96,112},{112,0},{1... | collective-permute-start | bytes 34568 | tf_op jit(solution)/shard_map/ppermute | solution.py:21
  164.4 5.6 %collective-permute-start.22 = (f32[60,48,1]{1,2,0:T(1,128)S(1)}, f32[60,48,1]{1,2,0:T(1,128)S(1)}, u32[]{:S(2)}, u32[]{:S(2)}) collective-permute-start(f32[60,48,1]{1,2,0:T(1,128)S(1)} %copy.253), channel_id=1, source_target_pairs={{16,0},{32,16},{48,32},{64,48},{80,64},{96,80},{112,96},{0,112},{1... | collective-permute-start | bytes 34568 | tf_op jit(solution)/shard_map/ppermute | solution.py:22
  164.4 14.5 %collective-permute-start.23 = (f32[60,1,128]{2,0,1:T(8,128)S(1)}, f32[60,1,128]{2,0,1:T(8,128)S(1)}, u32[]{:S(2)}, u32[]{:S(2)}) collective-permute-start(f32[60,1,128]{2,0,1:T(8,128)S(1)} %copy.271), channel_id=1, source_target_pairs={{0,1},{1,2},{2,3},{3,4},{4,5},{5,6},{6,7},{7,8},{8,9},{9,10},{10,1... | collective-permute-start | bytes 92168 | tf_op jit(solution)/shard_map/ppermute | solution.py:21
  168.7 10.2 %collective-permute-start.24 = (f32[60,1,128]{2,0,1:T(8,128)S(1)}, f32[60,1,128]{2,0,1:T(8,128)S(1)}, u32[]{:S(2)}, u32[]{:S(2)}) collective-permute-start(f32[60,1,128]{2,0,1:T(8,128)S(1)} %copy.255), channel_id=1, source_target_pairs={{1,0},{2,1},{3,2},{4,3},{5,4},{6,5},{7,6},{8,7},{9,8},{10,9},{11,1... | collective-permute-start | bytes 92168 | tf_op jit(solution)/shard_map/ppermute | solution.py:22
  173.5 5.4 %collective-permute-start.26 = (f32[60,128]{1,0:T(8,128)S(1)}, f32[60,128]{1,0:T(8,128)S(1)}, u32[]{:S(2)}, u32[]{:S(2)}) collective-permute-start(f32[60,128]{1,0:T(8,128)S(1)} %collective-permute-done.25), channel_id=1, source_target_pairs={{0,32},{16,48},{32,0},{48,16},{64,96},{80,112},{96,64},{112,80},{1... | collective-permute-start | bytes 92168 | tf_op jit(solution)/shard_map/ppermute | solution.py:28
  178.9 6.2 %copy-start.9 = (f32[30,49,128]{2,1,0:T(8,128)S(1)}, f32[30,49,128]{2,1,0:T(8,128)}, u32[]{:S(2)}) copy-start(f32[30,49,128]{2,1,0:T(8,128)} %copy-done.7) | copy-start | bytes 2257924
  178.9 4.3 %collective-permute-start.27 = (f32[60,128]{1,0:T(8,128)S(1)}, f32[60,128]{1,0:T(8,128)S(1)}, u32[]{:S(2)}, u32[]{:S(2)}) collective-permute-start(f32[60,128]{1,0:T(8,128)S(1)} %collective-permute-done.26), channel_id=1, source_target_pairs={{0,64},{16,80},{32,96},{48,112},{64,0},{80,16},{96,32},{112,48},{1... | collective-permute-start | bytes 92168 | tf_op jit(solution)/shard_map/ppermute | solution.py:28
  190.5 45.2 %collective-permute-start.32 = (f32[60,128]{1,0:T(8,128)S(1)}, f32[60,128]{1,0:T(8,128)S(1)}, u32[]{:S(2)}, u32[]{:S(2)}) collective-permute-start(f32[60,128]{1,0:T(8,128)S(1)} %bitcast.511), channel_id=1, source_target_pairs={{0,16},{16,0},{32,48},{48,32},{64,80},{80,64},{96,112},{112,96},{1... | collective-permute-start | bytes 92168 | tf_op jit(solution)/shard_map/ppermute | solution.py:28
  196.1 37.8 %collective-permute-start.28 = (f32[60,48,1]{0,1,2:T(8,128)S(1)}, f32[60,48,1]{0,1,2:T(8,128)S(1)}, u32[]{:S(2)}, u32[]{:S(2)}) collective-permute-start(f32[60,48,1]{0,1,2:T(8,128)S(1)} %copy.256), channel_id=1, source_target_pairs={{0,16},{16,32},{32,48},{48,64},{64,80},{80,96},{96,112},{112,0},{1... | collective-permute-start | bytes 34568 | tf_op jit(solution)/shard_map/ppermute | solution.py:21
  197.0 35.2 %collective-permute-start.29 = (f32[60,48,1]{0,1,2:T(8,128)S(1)}, f32[60,48,1]{0,1,2:T(8,128)S(1)}, u32[]{:S(2)}, u32[]{:S(2)}) collective-permute-start(f32[60,48,1]{0,1,2:T(8,128)S(1)} %copy.257), channel_id=1, source_target_pairs={{16,0},{32,16},{48,32},{64,48},{80,64},{96,80},{112,96},{0,112},{1... | collective-permute-start | bytes 34568 | tf_op jit(solution)/shard_map/ppermute | solution.py:22
  225.4 15.8 %collective-permute-start.30 = (f32[60,1,128]{2,0,1:T(8,128)S(1)}, f32[60,1,128]{2,0,1:T(8,128)S(1)}, u32[]{:S(2)}, u32[]{:S(2)}) collective-permute-start(f32[60,1,128]{2,0,1:T(8,128)S(1)} %copy.270), channel_id=1, source_target_pairs={{0,1},{1,2},{2,3},{3,4},{4,5},{5,6},{6,7},{7,8},{8,9},{9,10},{10,1... | collective-permute-start | bytes 92168 | tf_op jit(solution)/shard_map/ppermute | solution.py:21
  230.9 10.2 %collective-permute-start.31 = (f32[60,1,128]{2,0,1:T(8,128)S(1)}, f32[60,1,128]{2,0,1:T(8,128)S(1)}, u32[]{:S(2)}, u32[]{:S(2)}) collective-permute-start(f32[60,1,128]{2,0,1:T(8,128)S(1)} %copy.259), channel_id=1, source_target_pairs={{1,0},{2,1},{3,2},{4,3},{5,4},{6,5},{7,6},{8,7},{9,8},{10,9},{11,1... | collective-permute-start | bytes 92168 | tf_op jit(solution)/shard_map/ppermute | solution.py:22
  235.7 5.5 %collective-permute-start.33 = (f32[60,128]{1,0:T(8,128)S(1)}, f32[60,128]{1,0:T(8,128)S(1)}, u32[]{:S(2)}, u32[]{:S(2)}) collective-permute-start(f32[60,128]{1,0:T(8,128)S(1)} %collective-permute-done.32), channel_id=1, source_target_pairs={{0,32},{16,48},{32,0},{48,16},{64,96},{80,112},{96,64},{112,80},{1... | collective-permute-start | bytes 92168 | tf_op jit(solution)/shard_map/ppermute | solution.py:28
  241.2 6.3 %copy-start.10 = (f32[30,49,128]{2,1,0:T(8,128)S(1)}, f32[30,49,128]{2,1,0:T(8,128)}, u32[]{:S(2)}) copy-start(f32[30,49,128]{2,1,0:T(8,128)} %copy-done.7) | copy-start | bytes 2257924
  241.2 6.3 %copy-start.12 = (f32[30,49,128]{2,1,0:T(8,128)S(1)}, f32[30,49,128]{2,1,0:T(8,128)}, u32[]{:S(2)}) copy-start(f32[30,49,128]{2,1,0:T(8,128)} %get-tuple-element.211) | copy-start | bytes 2257924
  241.2 4.3 %collective-permute-start.34 = (f32[60,128]{1,0:T(8,128)S(1)}, f32[60,128]{1,0:T(8,128)S(1)}, u32[]{:S(2)}, u32[]{:S(2)}) collective-permute-start(f32[60,128]{1,0:T(8,128)S(1)} %collective-permute-done.33), channel_id=1, source_target_pairs={{0,64},{16,80},{32,96},{48,112},{64,0},{80,16},{96,32},{112,48},{1... | collective-permute-start | bytes 92168 | tf_op jit(solution)/shard_map/ppermute | solution.py:28
  295.9 5.2 %copy-start.22 = (f32[48,128]{1,0:T(8,128)}, f32[48,128]{1,0:T(8,128)S(1)}, u32[]{:S(2)}) copy-start(f32[48,128]{1,0:T(8,128)S(1)} %get-tuple-element.154) | copy-start | bytes 73732
  295.9 5.2 %copy-start.23 = (f32[48,128]{1,0:T(8,128)}, f32[48,128]{1,0:T(8,128)S(1)}, u32[]{:S(2)}) copy-start(f32[48,128]{1,0:T(8,128)S(1)} %get-tuple-element.156) | copy-start | bytes 73732
  295.9 5.2 %copy-start.24 = (f32[48,128]{1,0:T(8,128)}, f32[48,128]{1,0:T(8,128)S(1)}, u32[]{:S(2)}) copy-start(f32[48,128]{1,0:T(8,128)S(1)} %get-tuple-element.157) | copy-start | bytes 73732
  296.0 5.2 %copy-start.25 = (f32[48,128]{1,0:T(8,128)}, f32[48,128]{1,0:T(8,128)S(1)}, u32[]{:S(2)}) copy-start(f32[48,128]{1,0:T(8,128)S(1)} %get-tuple-element.158) | copy-start | bytes 73732
  296.0 5.2 %copy-start.26 = (f32[48,128]{1,0:T(8,128)}, f32[48,128]{1,0:T(8,128)S(1)}, u32[]{:S(2)}) copy-start(f32[48,128]{1,0:T(8,128)S(1)} %get-tuple-element.160) | copy-start | bytes 73732
  296.0 5.2 %copy-start.27 = (f32[48,128]{1,0:T(8,128)}, f32[48,128]{1,0:T(8,128)S(1)}, u32[]{:S(2)}) copy-start(f32[48,128]{1,0:T(8,128)S(1)} %get-tuple-element.161) | copy-start | bytes 73732
  296.0 5.2 %copy-start.28 = (f32[48,128]{1,0:T(8,128)}, f32[48,128]{1,0:T(8,128)S(1)}, u32[]{:S(2)}) copy-start(f32[48,128]{1,0:T(8,128)S(1)} %get-tuple-element.162) | copy-start | bytes 73732
  296.0 5.2 %copy-start.29 = (f32[48,128]{1,0:T(8,128)}, f32[48,128]{1,0:T(8,128)S(1)}, u32[]{:S(2)}) copy-start(f32[48,128]{1,0:T(8,128)S(1)} %get-tuple-element.164) | copy-start | bytes 73732
  296.0 5.2 %copy-start.30 = (f32[48,128]{1,0:T(8,128)}, f32[48,128]{1,0:T(8,128)S(1)}, u32[]{:S(2)}) copy-start(f32[48,128]{1,0:T(8,128)S(1)} %get-tuple-element.165) | copy-start | bytes 73732
  296.0 5.2 %copy-start.31 = (f32[48,128]{1,0:T(8,128)}, f32[48,128]{1,0:T(8,128)S(1)}, u32[]{:S(2)}) copy-start(f32[48,128]{1,0:T(8,128)S(1)} %get-tuple-element.166) | copy-start | bytes 73732
  296.0 5.2 %copy-start.32 = (f32[48,128]{1,0:T(8,128)}, f32[48,128]{1,0:T(8,128)S(1)}, u32[]{:S(2)}) copy-start(f32[48,128]{1,0:T(8,128)S(1)} %get-tuple-element.170) | copy-start | bytes 73732
  296.0 5.2 %copy-start.33 = (f32[48,128]{1,0:T(8,128)}, f32[48,128]{1,0:T(8,128)S(1)}, u32[]{:S(2)}) copy-start(f32[48,128]{1,0:T(8,128)S(1)} %get-tuple-element.172) | copy-start | bytes 73732
  378.6 15.8 %copy-start.67 = (f32[2,1,48,128]{3,2,1,0:T(8,128)S(1)}, f32[2,1,48,128]{3,2,1,0:T(8,128)}, u32[]{:S(2)}) copy-start(f32[2,1,48,128]{3,2,1,0:T(8,128)} %get-tuple-element.121) | copy-start | bytes 147460
  378.6 17.1 %copy-start.66 = (f32[2,1,48,128]{3,2,1,0:T(8,128)S(1)}, f32[2,1,48,128]{3,2,1,0:T(8,128)}, u32[]{:S(2)}) copy-start(f32[2,1,48,128]{3,2,1,0:T(8,128)} %get-tuple-element.120) | copy-start | bytes 147460
  378.6 18.4 %copy-start.46 = (f32[48,128]{1,0:T(8,128)S(1)}, f32[48,128]{1,0:T(8,128)}, u32[]{:S(2)}) copy-start(f32[48,128]{1,0:T(8,128)} %copy-done.45) | copy-start | bytes 73732
  378.6 34.7 %all-to-all-start.1 = ((f32[128,16,128]{2,1,0:T(8,128)}), f32[128,16,128]{2,1,0:T(8,128)S(1)}, u32[]{:S(2)}, u32[]{:S(2)}) async-start(f32[128,16,128]{2,1,0:T(8,128)} %reshape.692), calls=%async_computation.1 | async-start | bytes 2097152 | tf_op jit(solution)/shard_map/all_to_all | solution.py:131
  395.1 18.6 %copy-start.73 = (s32[2048]{0:T(1024)S(1)}, s32[2048]{0:T(1024)}, u32[]{:S(2)}) copy-start(s32[2048]{0:T(1024)} %reshape_squeeze.11) | copy-start | bytes 24580
  395.1 18.7 %copy-start.76 = (s32[16,4]{0,1:T(4,128)S(1)}, s32[16,4]{0,1:T(4,128)}, u32[]{:S(2)}) copy-start(s32[16,4]{0,1:T(4,128)} %multiply_add_fusion) | copy-start | bytes 772
  (54 other events, 189.3 us)
where the time goes:
time: 421 us; the launch traced here: 418 us
  local copies, waits for them, and re-layouts  126 us (30%)
  starting transfers between devices  102 us (24%)
  matrix products  91.3 us (22%)
  other arithmetic  73.6 us (17%)
  waiting for transfers between devices  21.1 us (5%)
    dot_general x1, matrix products, shards(): jnp.einsum('sab,sfb->sfa', tiles, lifted, precision=lax.Precision.HIGHEST)  57 us
    ppermute x15, starting transfers between devices, partner_2(): lax.ppermute(value, axis, [(i, i ^ 1 << bit) for i in range(lax.axis_size...  38.1 us
    dot_general x1, matrix products, shards(): jnp.einsum('sab,sfa->sfb', tiles, arrived, precision=lax.Precision.HIGHEST)  31.2 us
    ppermute x10, starting transfers between devices, padded(): before = lax.ppermute(last, axis, up)  28.5 us
    select_n x1, local copies, waits for them, and re-layouts, shards(): jnp.take(weight_tiles[0], tile_index[0].reshape(slot_count), axis=0)  26.3 us
    gather x2, local copies, waits for them, and re-layouts, shards(): jnp.take(weight_tiles[0], tile_index[0].reshape(slot_count), axis=0)  19 us
    mul x5, other arithmetic, transport(): open_east[:, :-1] * open_east[:, 1:]  19 us
    all_to_all x1, starting transfers between devices, outbound(): lax.all_to_all(buffer, ('gx', 'gy'), split_axis=0, concat_axis=0, tiled=T...  15.8 us
  transfers between devices with their start and end apart: 37, of which 7 were waited for; matrix products, arithmetic and copies ran while one was open for 38% of the time, Pallas kernels for 0%

commit v1 on v0

v1 whole, which is shorter than its diff:
```python
import jax
import jax.numpy as jnp
from jax import lax
from jax.experimental import pallas as pl
from jax.experimental.pallas import tpu as pltpu
from jax.sharding import PartitionSpec as P

F32 = jnp.float32
BF16 = jnp.bfloat16
MESH = pl.DeviceIdType.MESH
NF, B, CAP, ADV = 4, 32, 16, 4
GX, GY = 8, 16
DEV = GX * GY
SLOTS = DEV * CAP
LO, LA, OY, AY, LN = 30, 16, 48, 16, 128
PL = 2 * LO
TOP = 8
CHUNKS, CW = 8, 256
STRIDE = 37


def iota(shape, dim):
    return lax.broadcasted_iota(jnp.int32, shape, dim)


def split(x):
    hi = x.astype(BF16)
    return hi, (x - hi.astype(F32)).astype(BF16)


def fields_to_blocks(fields, q):
    lane = iota(fields[0].shape, 1) >> 5
    out = jnp.zeros_like(fields[0])
    for f in range(NF):
        moved = pltpu.roll(fields[f], ((f - q) * B) % LN, 1) if f != q else fields[f]
        out = jnp.where(lane == f, moved, out)
    return out


def blocks_to_field(groups, f):
    lane = iota(groups[0].shape, 1) >> 5
    out = jnp.zeros_like(groups[0])
    for q in range(4):
        moved = pltpu.roll(groups[q], ((q - f) * B) % LN, 1) if f != q else groups[q]
        out = jnp.where(lane == q, moved, out)
    return out


def slot_rows(idx):
    spread = (iota((CAP, LN), 1) & (CAP - 1)) == iota((CAP, LN), 0)
    tiled = jnp.dot(idx.astype(F32).astype(BF16), spread.astype(F32).astype(BF16), preferred_element_type=F32)
    own = (iota((DEV, LN), 1) >> 4) == (iota((DEV, LN), 0) & 7)
    return jnp.sum(jnp.where(own, tiled, 0.0).reshape(16, 8, LN), axis=1)


def kernel(
    tr, ue, un, kap, land, atemp, akap, aflux, wts, tix, sbl, rbl,
    out_tr, out_air, out_sf,
    v, u, n, kv, land_v, sea_p, at_v, ak_v, af_v, w_v, ti_v, sb_v, rb_v,
    rows3, w2t, w2p, oh_t, oh_h, oh_b, g1, g2,
    send1, recv1, send2, recv2, xt, sp, st,
    rsend, rrecv, csend, crecv,
    c0, ce, cw, cn, cs, elim_r, elim_z, top_y, air_r, air_z, x_out,
    in_sem, out_sem, hs_sem, hr_sem, a_sem,
):
    gx = lax.axis_index("gx")
    gy = lax.axis_index("gy")
    me = gx * GY + gy

    pairs = (
        (aflux, af_v), (rbl.at[0], rb_v), (land, land_v), (tr, v.at[0, :, TOP:TOP + OY, :]), (ue, u), (un, n),
        (wts.at[0], w_v), (tix.at[0], ti_v), (sbl.at[0], sb_v), (kap, kv), (atemp, at_v), (akap, ak_v),
    )
    loads = [pltpu.make_async_copy(s, d, in_sem.at[i]) for i, (s, d) in enumerate(pairs)]
    for c in loads:
        c.start()

    barrier = pltpu.get_barrier_semaphore()

    def peer(i):
        o = lax.rem(i * STRIDE, DEV)
        px = lax.rem(gx + lax.div(o, 16), GX)
        yz = lax.rem(o, 16)
        py = lax.rem(lax.div(gy, 4) + lax.div(yz, 4), 4) * 4 + lax.rem(lax.rem(gy, 4) + lax.rem(yz, 4), 4)
        return px, py

    def greet(i, carry):
        px, py = peer(i)
        pl.semaphore_signal(barrier, inc=1, device_id=(px, py), device_id_type=MESH)
        return carry

    lax.fori_loop(1, DEV, greet, 0)

    lane48 = iota((OY, LN), 1)
    row48 = iota((OY, LN), 0)

    loads[0].wait()
    loads[1].wait()
    tgt = rb_v[...]
    tgt = jnp.where(tgt < 64, (tgt & 3) * AY + (tgt >> 2), -1)
    rows3[1] = slot_rows(tgt)
    air = [af_v[f] for f in range(NF)]
    blocks = jnp.concatenate([fields_to_blocks(air, q) for q in range(4)], axis=0)
    bhi, blo = split(blocks)
    blocks2 = jnp.concatenate([bhi, blo], axis=0)
    sub128 = iota((LN, LN), 0)

    def pick(g, carry):
        row = rows3[1, pl.ds(g, 1), :]
        hot = jnp.where((sub128 & 63).astype(F32) == row, 1.0, 0.0)
        oh_b[g] = hot[:64].astype(BF16)
        picked = jnp.dot(hot.T.astype(BF16), blocks2, preferred_element_type=F32)
        send1[pl.ds(g * 8, 8)] = picked.reshape(8, CAP, LN)
        return carry

    lax.fori_loop(0, 16, pick, 0)

    for i in (2, 3, 4, 5):
        loads[i].wait()
    sea = land_v[...].astype(F32)
    sea_p[TOP:TOP + OY, :] = sea

    def first_edges(l, carry):
        acc, accu = carry
        for t in range(2):
            p = t * LO + l
            x = v[0, p, TOP:TOP + OY, :]
            acc = jnp.where((lane48 >> 1) == p, pltpu.roll(x, 2 * p + 1, 1), acc)
            rsend[0, 0, pl.ds(p, 1), :] = x[OY - 1:OY]
            rsend[0, 1, pl.ds(p, 1), :] = x[0:1]
        accu = jnp.where(lane48 == l, pltpu.roll(u[l] * sea, l + 1, 1), accu)
        rsend[0, 0, pl.ds(PL + l, 1), :] = n[l, OY - 1:OY, :] * sea[OY - 1:OY]
        return acc, accu

    zero48 = jnp.zeros((OY, LN), F32)
    acc, accu = lax.fori_loop(0, LO, first_edges, (zero48, zero48))
    acc = jnp.where((lane48 >> 1) == PL, pltpu.roll(sea, 2 * PL + 1, 1), acc)
    csend[0, 0] = acc
    csend[0, 1] = accu
    rsend[0, 1, PL:96, :] = jnp.zeros((96 - PL, LN), F32)
    tail = jnp.where(iota((8, LN), 0) == 2, sea[OY - 1:OY], 0.0)
    rsend[0, 0, 88:96, :] = jnp.where(iota((8, LN), 0) < 2, rsend[0, 0, 88:96, :], tail)
    rsend[0, 1, 88:96, :] = jnp.where(iota((8, LN), 0) == 2, sea[0:1], 0.0)

    @pl.when(gy == 0)
    def _():
        for s in range(ADV):
            rrecv[s, 1] = jnp.zeros((96, LN), F32)

    pl.semaphore_wait(barrier, DEV - 1)

    east, west = lax.rem(gx + 1, GX), lax.rem(gx + GX - 1, GX)

    def lines(s):
        return 96 if s == 0 else 64

    def sides(s):
        return 2 if s == 0 else 1

    def row_copy(s, out, into, to):
        return pltpu.make_async_remote_copy(
            src_ref=rsend.at[s, out, 0:lines(s), :], dst_ref=rrecv.at[s, into, 0:lines(s), :],
            send_sem=hs_sem.at[s, out], recv_sem=hr_sem.at[s, into], device_id=to, device_id_type=MESH)

    def col_copy(s, out, into, to):
        return pltpu.make_async_remote_copy(
            src_ref=csend.at[s, 0:sides(s)], dst_ref=crecv.at[s, into, 0:sides(s)],
            send_sem=hs_sem.at[s, 2 + out], recv_sem=hr_sem.at[s, 2 + into], device_id=to, device_id_type=MESH)

    def send_edges(s):
        col_copy(s, 0, 0, (east, gy)).start()
        col_copy(s, 1, 1, (west, gy)).start()

        @pl.when(gy < GY - 1)
        def _():
            row_copy(s, 0, 1, (gx, gy + 1)).start()

        @pl.when(gy == GY - 1)
        def _():
            row_copy(s, 0, 0, (GX - 1 - gx, gy)).start()

        @pl.when(gy > 0)
        def _():
            row_copy(s, 1, 0, (gx, gy - 1)).start()

    flip = jnp.where(iota((LN, LN), 0) + iota((LN, LN), 1) == LN - 1, 1.0, 0.0)

    def await_edges(s):
        col_copy(s, 0, 0, (east, gy)).wait()
        col_copy(s, 1, 1, (west, gy)).wait()
        row_copy(s, 0, 0, (east, gy)).wait()

        @pl.when(gy > 0)
        def _():
            row_copy(s, 1, 1, (east, gy)).wait()

        @pl.when(gy == GY - 1)
        def _():
            rows = rrecv[s, 0, 0:lines(s), :]
            rrecv[s, 0, 0:lines(s), :] = jnp.dot(
                rows, flip, precision=lax.Precision.HIGHEST, preferred_element_type=F32)

    send_edges(0)

    def exchange_out(i, carry):
        px, py = peer(i)
        pltpu.make_async_remote_copy(
            src_ref=send1.at[px * GY + py], dst_ref=recv1.at[me], send_sem=a_sem.at[0], recv_sem=a_sem.at[1],
            device_id=(px, py), device_id_type=MESH).start()
        return carry

    lax.fori_loop(1, DEV, exchange_out, 0)
    recv1[me] = send1[me]

    for i in (6, 7, 8):
        loads[i].wait()
    rows3[0] = slot_rows(ti_v[...])
    snd = sb_v[...]
    rows3[2] = slot_rows(jnp.where(snd < 192, (snd & 3) * OY + (snd >> 2), -1))
    for c in range(8):
        whi, wlo = split(w_v[:, c * LN:(c + 1) * LN])
        both = jnp.concatenate([whi.astype(F32), wlo.astype(F32)], axis=0)
        w2t[0, c * LN:(c + 1) * LN, :] = both.T
    for b in range(B):
        w2t[1, b * B:(b + 1) * B, :] = w2t[0, pl.ds(b, B, stride=B), :]
    w2p[0] = w2t[0].astype(BF16)
    w2p[1] = w2t[1].astype(BF16)

    def hots(g, carry):
        rt = rows3[0, pl.ds(g, 1), :]
        oh_t[g] = jnp.where((sub128 & 63).astype(F32) == rt, 1.0, 0.0).astype(BF16)
        rs = rows3[2, pl.ds(g, 1), :]
        oh_h[g] = jnp.where(iota((256, LN), 0).astype(F32) == rs, 1.0, 0.0).astype(BF16)
        return carry

    lax.fori_loop(0, 16, hots, 0)

    def tiles(c, carry):
        hot = jnp.concatenate([oh_t[2 * c], oh_t[2 * c + 1]], axis=1)
        g1[c] = jnp.dot(w2p[0], hot, preferred_element_type=F32)
        g2[c] = jnp.dot(w2p[1], hot, preferred_element_type=F32)
        return carry

    lax.fori_loop(0, CHUNKS, tiles, 0)

    await_edges(0)

    def ghosts(s):
        even = (lane48 & 1) == 0
        return jnp.where(even, pltpu.roll(crecv[s, 1, 0], LN - 1, 1), pltpu.roll(crecv[s, 0, 0], 1, 1))

    gh = ghosts(0)
    last = lane48 == LN - 1
    first = lane48 == 0
    gsea = pltpu.roll(gh, LN - 1 - 2 * PL, 1)
    sea_e = jnp.where(last, gsea, pltpu.roll(sea, LN - 1, 1))
    sea_p[TOP + OY:TOP + OY + 1, :] = rrecv[0, 0, 90:91, :]
    sea_n = sea_p[TOP + 1:TOP + 1 + OY, :]
    open_e = sea * sea_e
    open_n = sea * sea_n
    uw_ghost = crecv[0, 0, 1] * jnp.broadcast_to(sea[:, 0:1], (OY, LN))

    def faces(l, carry):
        um = u[l] * open_e
        uw = jnp.where(first, pltpu.roll(uw_ghost, lax.rem(LN - l, LN), 1), pltpu.roll(um, 1, 1))
        nm = n[l] * open_n
        below = rrecv[0, 1, pl.ds(PL + l, 1), :] * sea[0:1]
        ns = jnp.where(row48 == 0, below, pltpu.roll(nm, 1, 0))
        ce[l] = -jnp.minimum(um, 0.0)
        cw[l] = jnp.maximum(uw, 0.0)
        cn[l] = -jnp.minimum(nm, 0.0)
        cs[l] = jnp.maximum(ns, 0.0)
        c0[l] = 1.0 - jnp.maximum(um, 0.0) + jnp.minimum(uw, 0.0) - jnp.maximum(nm, 0.0) + jnp.minimum(ns, 0.0)
        return carry

    lax.fori_loop(0, LO, faces, 0)

    for s in range(ADV):
        if s > 0:
            await_edges(s)
        gh = ghosts(s)
        now, later = s % 2, (s + 1) % 2

        def substep(l, acc, s=s, now=now, later=later, gh=gh):
            k0, ke, kw, kn, ks = c0[l], ce[l], cw[l], cn[l], cs[l]
            for t in range(2):
                p = t * LO + l
                v[now, p, TOP - 1:TOP, :] = rrecv[s, 1, pl.ds(p, 1), :]
                v[now, p, TOP + OY:TOP + OY + 1, :] = rrecv[s, 0, pl.ds(p, 1), :]
                x = v[now, p, TOP:TOP + OY, :]
                g = pltpu.roll(gh, LN - 1 - 2 * p, 1)
                xe = jnp.where(last, g, pltpu.roll(x, LN - 1, 1))
                xw = jnp.where(first, g, pltpu.roll(x, 1, 1))
                y = k0 * x + ke * xe + kw * xw
                y = y + kn * v[now, p, TOP + 1:TOP + 1 + OY, :] + ks * v[now, p, TOP - 1:TOP - 1 + OY, :]
                v[later, p, TOP:TOP + OY, :] = y
                if s < ADV - 1:
                    acc = jnp.where((lane48 >> 1) == p, pltpu.roll(y, 2 * p + 1, 1), acc)
                    rsend[s + 1, 0, pl.ds(p, 1), :] = y[OY - 1:OY]
                    rsend[s + 1, 1, pl.ds(p, 1), :] = y[0:1]
            return acc

        acc = lax.fori_loop(0, LO, substep, zero48)
        if s < ADV - 1:
            csend[s + 1, 0] = acc
            for k in range(2):
                rsend[s + 1, k, PL:64, :] = jnp.zeros((64 - PL, LN), F32)
            send_edges(s + 1)

    loads[9].wait()

    def up(i, carry):
        e, yt, ys = carry
        l = LO - 2 - i
        k = kv[l] * sea
        inv = 1.0 / (e + k)
        r = k * inv
        elim_r[l + 1] = r
        elim_z[0, l + 1] = yt * inv
        elim_z[1, l + 1] = ys * inv
        return (1.0 + k * (1.0 - r), v[0, l, TOP:TOP + OY, :] + r * yt, v[0, LO + l, TOP:TOP + OY, :] + r * ys)

    start = (jnp.ones((OY, LN), F32), v[0, LO - 1, TOP:TOP + OY, :], v[0, PL - 1, TOP:TOP + OY, :])
    e, yt, ys = lax.fori_loop(0, LO - 1, up, start)
    inv = 1.0 / e
    top_y[0], top_y[1], top_y[2] = yt, ys, inv

    loads[10].wait()
    loads[11].wait()

    def air_up(i, carry):
        e, y = carry
        l = LA - 2 - i
        k = ak_v[l + 1]
        inv = 1.0 / (e + k)
        r = k * inv
        air_r[l + 1] = r
        air_z[l + 1] = y * inv
        return 1.0 + k * (1.0 - r), at_v[l] + r * y

    ea, ya = lax.fori_loop(0, LA - 1, air_up, (jnp.ones((AY, LN), F32), at_v[LA - 1]))
    inv_a = 1.0 / (ea + ak_v[0])
    air_z[0] = ya
    air_r[0] = inv_a

    def exchange_wait(snd_buf, rcv_buf, k):
        return pltpu.make_async_remote_copy(
            src_ref=snd_buf.at[pl.ds(0, DEV - 1)], dst_ref=rcv_buf.at[pl.ds(0, DEV - 1)],
            send_sem=a_sem.at[2 * k], recv_sem=a_sem.at[2 * k + 1], device_id=(east, gy), device_id_type=MESH)

    exchange_wait(send1, recv1, 0).wait_recv()

    def apply_tiles(tile_ref, c, h):
        total = jnp.zeros((NF, B, LN), F32)
        for a in range(B):
            w = tile_ref[c, a * B:(a + 1) * B, h * LN:(h + 1) * LN]
            total = total + w[None] * xt[:, a:a + 1, :]
        return total.reshape(NF * B, LN)

    def spread(c, carry):
        for h in range(2):
            xt[...] = recv1[pl.ds(c * 16 + h * 8, 8)].reshape(LN, LN).T.reshape(NF, B, LN)
            hi, lo = split(apply_tiles(g1, c, h))
            sp[2 * c + h, 0:LN, :] = hi
            sp[2 * c + h, LN:, :] = lo
        return carry

    lax.fori_loop(0, CHUNKS, spread, 0)

    def collect(g, total):
        return total + lax.dot_general(
            oh_h[g, 0:192, :], sp[g], (((1,), (1,)), ((), ())), preferred_element_type=F32)

    both = lax.fori_loop(0, 16, collect, jnp.zeros((192, 256), F32))
    landed = both[:, :LN] + both[:, LN:]
    groups = [landed[q * OY:(q + 1) * OY] for q in range(4)]
    force = [blocks_to_field(groups, f) for f in range(NF)]

    xt0 = (top_y[0] + sea * force[0]) * top_y[2]
    xs0 = (top_y[1] + sea * force[1]) * top_y[2]
    surf = [
        sea * xt0,
        sea,
        sea * (u[0] + 0.1 * jnp.tanh(force[2])),
        sea * (n[0] + 0.1 * jnp.tanh(force[3])),
    ]
    sblocks = jnp.concatenate([fields_to_blocks(surf, q) for q in range(4)] + [jnp.zeros((64, LN), F32)], axis=0)
    lifted = jnp.concatenate([sblocks[:LN].T, sblocks[LN:].T], axis=1)
    lhi, llo = split(lifted)
    st[...] = jnp.concatenate([lhi, llo], axis=0)

    def push(i, carry):
        c = lax.rem(gx + 1 + i, GX)
        for h in range(2):
            g = 2 * c + h
            two = jnp.dot(st[...], oh_h[g], preferred_element_type=F32)
            xt[...] = (two[:LN] + two[LN:]).reshape(NF, B, LN)
            send2[pl.ds(g * 8, 8)] = apply_tiles(g2, c, h).T.reshape(8, CAP, LN)

        def out(j, carry2):
            py = lax.rem(gy + j, GY)
            copy = pltpu.make_async_remote_copy(
                src_ref=send2.at[c * GY + py], dst_ref=recv2.at[me], send_sem=a_sem.at[2], recv_sem=a_sem.at[3],
                device_id=(c, py), device_id_type=MESH)
            copy.start()
            return carry2

        @pl.when(i < GX - 1)
        def _():
            lax.fori_loop(0, GY, out, 0)

        @pl.when(i == GX - 1)
        def _():
            lax.fori_loop(1, GY, out, 0)

        return carry

    lax.fori_loop(0, GX, push, 0)
    recv2[me] = send2[me]

    x_out[0] = xt0
    x_out[LO] = xs0

    def down(l, carry):
        a, b = carry
        r = elim_r[l]
        a = elim_z[0, l] + r * a
        b = elim_z[1, l] + r * b
        x_out[l] = a
        x_out[LO + l] = b
        return a, b

    lax.fori_loop(1, LO, down, (xt0, xs0))
    store = pltpu.make_async_copy(x_out, out_tr, out_sem)
    store.start()

    exchange_wait(send2, recv2, 1).wait_recv()

    def gather(g, total):
        hi, lo = split(recv2[pl.ds(g * 8, 8)].reshape(LN, LN))
        return total + jnp.dot(oh_b[g], jnp.concatenate([hi, lo], axis=1), preferred_element_type=F32)

    both = lax.fori_loop(0, 16, gather, jnp.zeros((64, 256), F32))
    landed = both[:, :LN] + both[:, LN:]
    groups = [landed[q * AY:(q + 1) * AY] for q in range(4)]
    fields = [blocks_to_field(groups, f) for f in range(NF)]
    for f in range(NF):
        out_sf[f] = fields[f]
    ground = at_v[0] * (1.0 - fields[1]) + fields[0]
    x = (air_z[0] + ak_v[0] * ground) * air_r[0]
    out_air[0] = x
    for l in range(1, LA):
        x = air_z[l] + air_r[l] * x
        out_air[l] = x

    for s in range(ADV):
        pass
    exchange_wait(send1, recv1, 0).wait_send()
    exchange_wait(send2, recv2, 1).wait_send()
    store.wait()


def shards(
    tracers, east_flow, north_flow, ocean_kappa, land_sea, air_temp, air_kappa, air_fluxes,
    weight_tiles, tile_index, send_blocks, receive_blocks,
):
    anyspace = pl.BlockSpec(memory_space=pl.ANY)
    vm = pl.BlockSpec(memory_space=pltpu.VMEM)
    V = pltpu.VMEM
    scratch = [
        V((2, PL, 64, LN), F32), V((LO, OY, LN), F32), V((LO, OY, LN), F32), V((LO - 1, OY, LN), F32),
        V((OY, LN), jnp.int32), V((64, LN), F32), V((LA, AY, LN), F32), V((LA, AY, LN), F32), V((NF, AY, LN), F32),
        V((64, 1024), F32), V((DEV, CAP), jnp.int32), V((DEV, CAP), jnp.int32), V((DEV, CAP), jnp.int32),
        V((3, 16, LN), F32), V((2, 1024, LN), F32), V((2, 1024, LN), BF16),
        V((16, LN, LN), BF16), V((16, 256, LN), BF16), V((16, 64, LN), BF16),
        V((CHUNKS, 1024, CW), F32), V((CHUNKS, 1024, CW), F32),
        V((DEV, CAP, LN), F32), V((DEV, CAP, LN), F32), V((DEV, CAP, LN), F32), V((DEV, CAP, LN), F32),
        V((NF, B, LN), F32), V((16, 256, LN), BF16), V((256, 256), BF16),
        V((ADV, 2, 96, LN), F32), V((ADV, 2, 96, LN), F32), V((ADV, 2, OY, LN), F32), V((ADV, 2, 2, OY, LN), F32),
        V((LO, OY, LN), F32), V((LO, OY, LN), F32), V((LO, OY, LN), F32), V((LO, OY, LN), F32), V((LO, OY, LN), F32),
        V((LO, OY, LN), F32), V((2, LO, OY, LN), F32), V((3, OY, LN), F32), V((LA, AY, LN), F32), V((LA, AY, LN), F32),
        V((PL, OY, LN), F32),
        pltpu.SemaphoreType.DMA((12,)), pltpu.SemaphoreType.DMA, pltpu.SemaphoreType.DMA((ADV, 4)),
        pltpu.SemaphoreType.DMA((ADV, 4)), pltpu.SemaphoreType.DMA((4,)),
    ]
    out_tr, out_air, out_sf = pl.pallas_call(
        kernel,
        out_shape=(
            jax.ShapeDtypeStruct((PL, OY, LN), F32),
            jax.ShapeDtypeStruct((LA, AY, LN), F32),
            jax.ShapeDtypeStruct((NF, AY, LN), F32),
        ),
        in_specs=[anyspace] * 12,
        out_specs=(anyspace, vm, vm),
        scratch_shapes=scratch,
        compiler_params=pltpu.CompilerParams(
            collective_id=0, has_side_effects=True, vmem_limit_bytes=56 * 1024 * 1024),
        name="coupling_step",
    )(
        tracers.reshape(PL, OY, LN), east_flow, north_flow, ocean_kappa, land_sea, air_temp, air_kappa, air_fluxes,
        weight_tiles, tile_index, send_blocks, receive_blocks,
    )
    return out_tr.reshape(2, LO, OY, LN), out_air, out_sf


def solution(mesh):
    return jax.shard_map(
        shards,
        mesh=mesh,
        in_specs=(
            P(None, None, "gy", "gx"),
            P(None, "gy", "gx"),
            P(None, "gy", "gx"),
            P(None, "gy", "gx"),
            P("gy", "gx"),
            P(None, "gy", "gx"),
            P(None, "gy", "gx"),
            P(None, "gy", "gx"),
            P(("gx", "gy"), None, None),
            P(("gx", "gy"), None, None),
            P(("gx", "gy"), None, None),
            P(("gx", "gy"), None, None),
        ),
        out_specs=(P(None, None, "gy", "gx"), P(None, "gy", "gx"), P(None, "gy", "gx")),
        check_vma=False,
    )
```

time: 421 us -> 96 us (0.23)
  local copies, waits for them, and re-layouts: 126 us -> 8.15 us
  starting transfers between devices: 102 us -> 0 us
  matrix products: 91.3 us -> 0 us
  Pallas kernels: 0 us -> 86.9 us
  other arithmetic: 73.6 us -> 0 us
  waiting for transfers between devices: 21.1 us -> 0 us
    dot_general x4 -> x0, matrix products: 91.3 us -> none  [the longest x1 57 us: shards(): jnp.einsum('sab,sfb->sfa', tiles, lifted, precision=lax.Precision.HIGHEST)]
    pallas_call x0 -> x1, Pallas kernels: none -> 86.9 us  [shards(): pl.pallas_call(kernel, out_shape=(jax.ShapeDtypeStruct((PL, OY, LN), F32)...]
    ppermute x35 -> x0, starting transfers between devices: 73.6 us -> none  [the longest x15 38.1 us: partner_2(): lax.ppermute(value, axis, [(i, i ^ 1 << bit) for i in range(lax.axis_size...]
    gather x5 -> x0, local copies, waits for them, and re-layouts: 31.2 us -> none  [the longest x2 19 us: shards(): jnp.take(weight_tiles[0], tile_index[0].reshape(slot_count), axis=0)]
    mul x12 -> x0, other arithmetic: 30.2 us -> none  [the longest x5 19 us: transport(): open_east[:, :-1] * open_east[:, 1:]]
    select_n x2 -> x0, local copies, waits for them, and re-layouts: 29.4 us -> none  [the longest x1 26.3 us: shards(): jnp.take(weight_tiles[0], tile_index[0].reshape(slot_count), axis=0)]
    all_to_all x2 -> x0, starting transfers between devices: 28.8 us -> none  [the longest x1 15.8 us: outbound(): lax.all_to_all(buffer, ('gx', 'gy'), split_axis=0, concat_axis=0, tiled=T...]
    all_to_all x2 -> x0, waiting for transfers between devices: 15.1 us -> none  [the longest x1 15.1 us: outbound(): lax.all_to_all(buffer, ('gx', 'gy'), split_axis=0, concat_axis=0, tiled=T...]
  transfers between devices with their start and end apart: 37 -> 0, of which waited for: 7 -> 0; matrix products, arithmetic and copies ran while one was open for 38% -> 0% of each run, Pallas kernels for 0% -> 0%
where the time goes in v1:
time: 96 us; the launch traced here: 95.7 us
  Pallas kernels  86.9 us (91%)
  local copies, waits for them, and re-layouts  8.15 us (8%)
    pallas_call x1, Pallas kernels, shards(): pl.pallas_call(kernel, out_shape=(jax.ShapeDtypeStruct((PL, OY, LN), F32)...  86.9 us
    unnamed x10, local copies, waits for them, and re-layouts  8.15 us

profile of v1, /device:TPU:1, one launch (start us, length us, event | category | flops | bytes accessed | tf_op | source)
XLA Modules:
  0.0 95.7 jit_solution(51744224350856026)
XLA Ops:
  0.6 1.4 %copy.15.tix = s32[1,128,16]{2,1,0:T(8,128)} copy(s32[1,128,16]{1,2,0:T(8,128)} %param.21) | data formatting | bytes 16384 | tf_op args[9]
  2.1 1.4 %copy.16.sbl = s32[1,128,16]{2,1,0:T(8,128)} copy(s32[1,128,16]{1,2,0:T(8,128)} %param.22) | data formatting | bytes 16384 | tf_op args[10]
  3.5 1.4 %copy.17.rbl = s32[1,128,16]{2,1,0:T(8,128)} copy(s32[1,128,16]{1,2,0:T(8,128)} %param.23) | data formatting | bytes 16384 | tf_op args[11]
  4.9 86.9 %coupling_step.1 = (f32[60,48,128]{2,1,0:T(8,128)}, f32[16,16,128]{2,1,0:T(8,128)}, f32[4,16,128]{2,1,0:T(8,128)}) custom-call(f32[60,48,128]{2,1,0:T(8,128)} %bitcast.2, f32[30,48,128]{2,1,0:T(8,128)} %ue.1, f32[30,48,128]{2,1,0:T(8,128)} %un.1, f32[29,48,128]{2,1,0:T(8,128)} %kap.1, s32[48,128]{1,0:T(8,128)} %land.1, f32[16,16,128]{2,1,0:T(8,128)} %atemp.1, ...), custom_call_target="tpu_custom_call" | custom-call | tf_op jit(solution)/shard_map/coupling_step/pallas_call | solution.py:486
  91.8 0.0 copy-start
  91.8 0.0 copy-start.1
  91.8 2.6 %copy.21 = f32[2,30,48,128]{3,2,1,0:T(8,128)} copy(f32[2,30,48,128]{3,2,1,0:T(8,128)} %bitcast.3) | data formatting | bytes 2949120
  94.4 0.0 copy-done
  94.5 0.7 copy.22
  95.1 0.0 copy-done.1
  95.1 0.6 copy.23
Async XLA Ops:
  91.8 2.6 %copy-start = (f32[16,16,128]{2,1,0:T(8,128)S(1)}, f32[16,16,128]{2,1,0:T(8,128)}, u32[]{:S(2)}) copy-start(f32[16,16,128]{2,1,0:T(8,128)} %get-tuple-element.13) | copy-start | bytes 393220
  91.8 3.3 %copy-start.1 = (f32[4,16,128]{2,1,0:T(8,128)S(1)}, f32[4,16,128]{2,1,0:T(8,128)}, u32[]{:S(2)}) copy-start(f32[4,16,128]{2,1,0:T(8,128)} %get-tuple-element.14) | copy-start | bytes 98308

commit v2 on v1

--- a/solution.py
+++ b/solution.py
@@ -16,7 +16,9 @@
 PL = 2 * LO
 TOP = 8
 CHUNKS, CW = 8, 256
-STRIDE = 37
+GROUP = 5
+SENDS = (3, 2, 2, 1)
+PARTS = 6
 
 
 def iota(shape, dim):
@@ -48,7 +50,7 @@
 
 def slot_rows(idx):
     spread = (iota((CAP, LN), 1) & (CAP - 1)) == iota((CAP, LN), 0)
-    tiled = jnp.dot(idx.astype(F32).astype(BF16), spread.astype(F32).astype(BF16), preferred_element_type=F32)
+    tiled = jnp.dot(idx.astype(F32).T.astype(BF16), spread.astype(F32).astype(BF16), preferred_element_type=F32)
     own = (iota((DEV, LN), 1) >> 4) == (iota((DEV, LN), 0) & 7)
     return jnp.sum(jnp.where(own, tiled, 0.0).reshape(16, 8, LN), axis=1)
 
@@ -56,20 +58,21 @@
 def kernel(
     tr, ue, un, kap, land, atemp, akap, aflux, wts, tix, sbl, rbl,
     out_tr, out_air, out_sf,
-    v, u, n, kv, land_v, sea_p, at_v, ak_v, af_v, w_v, ti_v, sb_v, rb_v,
-    rows3, w2t, w2p, oh_t, oh_h, oh_b, g1, g2,
-    send1, recv1, send2, recv2, xt, sp, st,
+    va, vb, xs, w_shift, w_ghost, w_edge, u, n, kv, land_v, sea_p, at_v, ak_v, af_v, w_v, ti_v, sb_v, rb_v,
+    rows3, w2t, w2p, oh_t, oh_h, oh_ht, oh_b, g1, g2,
+    send1, recv1, send2, recv2, xt, total, st,
     rsend, rrecv, csend, crecv,
     c0, ce, cw, cn, cs, elim_r, elim_z, top_y, air_r, air_z, x_out,
-    in_sem, out_sem, hs_sem, hr_sem, a_sem,
+    in_sem, out_sem, hs_sem, hr_sem, as_sem, ar_sem,
 ):
     gx = lax.axis_index("gx")
     gy = lax.axis_index("gy")
     me = gx * GY + gy
 
     pairs = (
-        (aflux, af_v), (rbl.at[0], rb_v), (land, land_v), (tr, v.at[0, :, TOP:TOP + OY, :]), (ue, u), (un, n),
+        (aflux, af_v), (rbl.at[0], rb_v), (land, land_v), (tr.at[0], va.at[:, 0, TOP:TOP + OY, :]), (ue, u), (un, n),
         (wts.at[0], w_v), (tix.at[0], ti_v), (sbl.at[0], sb_v), (kap, kv), (atemp, at_v), (akap, ak_v),
+        (tr.at[1], va.at[:, 1, TOP:TOP + OY, :]),
     )
     loads = [pltpu.make_async_copy(s, d, in_sem.at[i]) for i, (s, d) in enumerate(pairs)]
     for c in loads:
@@ -77,16 +80,10 @@
 
     barrier = pltpu.get_barrier_semaphore()
 
-    def peer(i):
-        o = lax.rem(i * STRIDE, DEV)
-        px = lax.rem(gx + lax.div(o, 16), GX)
-        yz = lax.rem(o, 16)
-        py = lax.rem(lax.div(gy, 4) + lax.div(yz, 4), 4) * 4 + lax.rem(lax.rem(gy, 4) + lax.rem(yz, 4), 4)
-        return px, py
-
     def greet(i, carry):
-        px, py = peer(i)
-        pl.semaphore_signal(barrier, inc=1, device_id=(px, py), device_id_type=MESH)
+        pl.semaphore_signal(
+            barrier, inc=1, device_id=(lax.rem(gx + lax.div(i, GY), GX), lax.rem(gy + lax.rem(i, GY), GY)),
+            device_id_type=MESH)
         return carry
 
     lax.fori_loop(1, DEV, greet, 0)
@@ -115,25 +112,49 @@
 
     lax.fori_loop(0, 16, pick, 0)
 
-    for i in (2, 3, 4, 5):
+    for i in (2, 3, 4, 5, 12):
         loads[i].wait()
     sea = land_v[...].astype(F32)
     sea_p[TOP:TOP + OY, :] = sea
 
-    def first_edges(l, carry):
-        acc, accu = carry
-        for t in range(2):
-            p = t * LO + l
-            x = v[0, p, TOP:TOP + OY, :]
-            acc = jnp.where((lane48 >> 1) == p, pltpu.roll(x, 2 * p + 1, 1), acc)
-            rsend[0, 0, pl.ds(p, 1), :] = x[OY - 1:OY]
-            rsend[0, 1, pl.ds(p, 1), :] = x[0:1]
-        accu = jnp.where(lane48 == l, pltpu.roll(u[l] * sea, l + 1, 1), accu)
-        rsend[0, 0, pl.ds(PL + l, 1), :] = n[l, OY - 1:OY, :] * sea[OY - 1:OY]
-        return acc, accu
+    src, dst = iota((256, 256), 0) & (LN - 1), iota((256, 256), 1)
+    to_east = (src == dst + 1) & (dst < LN - 1)
+    to_west = (src == dst - 1 - LN) & (dst > LN)
+    w_shift[...] = jnp.where(to_east | to_west, 1.0, 0.0).astype(BF16)
+    even = (src & 1) == 0
+    w_ghost[...] = jnp.where((even & (dst == LN - 1)) | ((src & 1 == 1) & (dst == LN)), 1.0, 0.0).astype(BF16)
+    src, dst = iota((256, LN), 0) & (LN - 1), iota((256, LN), 1)
+    even = (dst & 1) == 0
+    w_edge[...] = jnp.where((even & (src == LN - 1)) | ((dst & 1 == 1) & (src == 0)), 1.0, 0.0).astype(BF16)
+
+    def keep(p, x):
+        xs[pl.ds(pl.multiple_of(p * OY, OY), OY), :] = jnp.concatenate(split(x), axis=1)
+
+    def group_rows(i):
+        return pl.ds(pl.multiple_of(i * (2 * GROUP * OY), 2 * GROUP * OY), 2 * GROUP * OY)
+
+    def edge_columns(i, acc):
+        found = jnp.dot(xs[group_rows(i), :], w_edge[...], preferred_element_type=F32)
+        for k in range(2 * GROUP):
+            acc = jnp.where((lane48 >> 1) == i * 2 * GROUP + k, found[k * OY:(k + 1) * OY], acc)
+        return acc
+
+    def first_edges(i, accu):
+        for j in range(GROUP):
+            l = i * GROUP + j
+            for t in range(2):
+                p = 2 * l + t
+                x = va[l, t, TOP:TOP + OY, :]
+                keep(p, x)
+                rsend[0, 0, pl.ds(p, 1), :] = x[OY - 1:OY]
+                rsend[0, 1, pl.ds(p, 1), :] = x[0:1]
+            accu = jnp.where(lane48 == l, pltpu.roll(u[l] * sea, l + 1, 1), accu)
+            rsend[0, 0, pl.ds(PL + l, 1), :] = n[l, OY - 1:OY, :] * sea[OY - 1:OY]
+        return accu
 
     zero48 = jnp.zeros((OY, LN), F32)
-    acc, accu = lax.fori_loop(0, LO, first_edges, (zero48, zero48))
+    accu = lax.fori_loop(0, LO // GROUP, first_edges, zero48)
+    acc = lax.fori_loop(0, LO // GROUP, edge_columns, zero48)
     acc = jnp.where((lane48 >> 1) == PL, pltpu.roll(sea, 2 * PL + 1, 1), acc)
     csend[0, 0] = acc
     csend[0, 1] = accu
@@ -202,14 +223,53 @@
 
     send_edges(0)
 
+    def exchange_copy(k, snd_buf, rcv_buf, px, py):
+        return pltpu.make_async_remote_copy(
+            src_ref=snd_buf.at[px * GY + py], dst_ref=rcv_buf.at[me], send_sem=as_sem.at[k], recv_sem=ar_sem.at[k, gx],
+            device_id=(px, py), device_id_type=MESH)
+
+    def send_chunk(k, snd_buf, rcv_buf, c, start):
+        def out(j, carry):
+            exchange_copy(k, snd_buf, rcv_buf, c, lax.rem(gy + j, GY)).start()
+            return carry
+
+        lax.fori_loop(start, GY, out, 0)
+
+    def exchange_wait(k, snd_buf, rcv_buf, c, blocks):
+        return pltpu.make_async_remote_copy(
+            src_ref=snd_buf.at[pl.ds(0, blocks)], dst_ref=rcv_buf.at[pl.ds(0, blocks)],
+            send_sem=as_sem.at[k], recv_sem=ar_sem.at[k, c], device_id=(east, gy), device_id_type=MESH)
+
+    def chunk_order(i):
+        return lax.rem(gx + 1 + i, GX)
+
+    def arrival_order(i):
+        return lax.rem(gx + GX - 1 - i, GX)
+
+    def await_chunk(k, snd_buf, rcv_buf, i):
+        c = arrival_order(i)
+
+        @pl.when(i < GX - 1)
+        def _():
+            exchange_wait(k, snd_buf, rcv_buf, c, GY).wait_recv()
+
+        @pl.when(i == GX - 1)
+        def _():
+            exchange_wait(k, snd_buf, rcv_buf, c, GY - 1).wait_recv()
+
+        return c
+
     def exchange_out(i, carry):
-        px, py = peer(i)
-        pltpu.make_async_remote_copy(
-            src_ref=send1.at[px * GY + py], dst_ref=recv1.at[me], send_sem=a_sem.at[0], recv_sem=a_sem.at[1],
-            device_id=(px, py), device_id_type=MESH).start()
-        return carry
-
-    lax.fori_loop(1, DEV, exchange_out, 0)
+        send_chunk(0, send1, recv1, chunk_order(i), 0)
+        return carry
+
+    def exchange_part(s):
+        begin, end = sum(SENDS[:s]), sum(SENDS[:s + 1])
+        lax.fori_loop(begin, min(end, GX - 1), exchange_out, 0)
+        if end == GX and SENDS[s] > 0:
+            send_chunk(0, send1, recv1, gx, 1)
+
+    exchange_part(0)
     recv1[me] = send1[me]
 
     for i in (6, 7, 8):
@@ -230,7 +290,10 @@
         rt = rows3[0, pl.ds(g, 1), :]
         oh_t[g] = jnp.where((sub128 & 63).astype(F32) == rt, 1.0, 0.0).astype(BF16)
         rs = rows3[2, pl.ds(g, 1), :]
-        oh_h[g] = jnp.where(iota((256, LN), 0).astype(F32) == rs, 1.0, 0.0).astype(BF16)
+        hot = jnp.where(iota((256, LN), 0).astype(F32) == rs, 1.0, 0.0)
+        oh_h[g] = hot.astype(BF16)
+        oh_ht[g, :, 0:LN] = hot[:LN].T.astype(BF16)
+        oh_ht[g, :, LN:] = hot[LN:].T.astype(BF16)
         return carry
 
     lax.fori_loop(0, 16, hots, 0)
@@ -241,9 +304,10 @@
         g2[c] = jnp.dot(w2p[1], hot, preferred_element_type=F32)
         return carry
 
-    lax.fori_loop(0, CHUNKS, tiles, 0)
+    lax.fori_loop(0, 2, tiles, 0)
 
     await_edges(0)
+
 
     def ghosts(s):
         even = (lane48 & 1) == 0
@@ -260,7 +324,12 @@
     open_n = sea * sea_n
     uw_ghost = crecv[0, 0, 1] * jnp.broadcast_to(sea[:, 0:1], (OY, LN))
 
-    def faces(l, carry):
+    def faces(i, carry):
+        for j in range(GROUP):
+            face(i * GROUP + j)
+        return carry
+
+    def face(l):
         um = u[l] * open_e
         uw = jnp.where(first, pltpu.roll(uw_ghost, lax.rem(LN - l, LN), 1), pltpu.roll(um, 1, 1))
         nm = n[l] * open_n
@@ -271,41 +340,58 @@
         cn[l] = -jnp.minimum(nm, 0.0)
         cs[l] = jnp.maximum(ns, 0.0)
         c0[l] = 1.0 - jnp.maximum(um, 0.0) + jnp.minimum(uw, 0.0) - jnp.maximum(nm, 0.0) + jnp.minimum(ns, 0.0)
-        return carry
-
-    lax.fori_loop(0, LO, faces, 0)
+
+    lax.fori_loop(0, LO // GROUP, faces, 0)
 
     for s in range(ADV):
         if s > 0:
+            lax.fori_loop(2 * s, 2 * s + 2, tiles, 0)
             await_edges(s)
         gh = ghosts(s)
-        now, later = s % 2, (s + 1) % 2
-
-        def substep(l, acc, s=s, now=now, later=later, gh=gh):
-            k0, ke, kw, kn, ks = c0[l], ce[l], cw[l], cn[l], cs[l]
-            for t in range(2):
-                p = t * LO + l
-                v[now, p, TOP - 1:TOP, :] = rrecv[s, 1, pl.ds(p, 1), :]
-                v[now, p, TOP + OY:TOP + OY + 1, :] = rrecv[s, 0, pl.ds(p, 1), :]
-                x = v[now, p, TOP:TOP + OY, :]
-                g = pltpu.roll(gh, LN - 1 - 2 * p, 1)
-                xe = jnp.where(last, g, pltpu.roll(x, LN - 1, 1))
-                xw = jnp.where(first, g, pltpu.roll(x, 1, 1))
-                y = k0 * x + ke * xe + kw * xw
-                y = y + kn * v[now, p, TOP + 1:TOP + 1 + OY, :] + ks * v[now, p, TOP - 1:TOP - 1 + OY, :]
-                v[later, p, TOP:TOP + OY, :] = y
-                if s < ADV - 1:
-                    acc = jnp.where((lane48 >> 1) == p, pltpu.roll(y, 2 * p + 1, 1), acc)
-                    rsend[s + 1, 0, pl.ds(p, 1), :] = y[OY - 1:OY]
-                    rsend[s + 1, 1, pl.ds(p, 1), :] = y[0:1]
-            return acc
-
-        acc = lax.fori_loop(0, LO, substep, zero48)
+        now, later = (va, vb) if s % 2 == 0 else (vb, va)
+
+        def edges_in(i, carry, s=s, now=now):
+            for j in range(GROUP):
+                l = i * GROUP + j
+                for t in range(2):
+                    now[l, t, TOP - 1:TOP, :] = rrecv[s, 1, pl.ds(2 * l + t, 1), :]
+                    now[l, t, TOP + OY:TOP + OY + 1, :] = rrecv[s, 0, pl.ds(2 * l + t, 1), :]
+            return carry
+
+        lax.fori_loop(0, LO // GROUP, edges_in, 0)
+        ghi, glo = (x.astype(F32) for x in split(gh))
+
+        def substep(i, carry, s=s, now=now, later=later, ghi=ghi, glo=glo):
+            parts = []
+            for k in range(2 * GROUP):
+                own = (lane48 >> 1) == i * 2 * GROUP + k
+                parts.append(jnp.concatenate(
+                    [jnp.where(own, ghi, 0.0).astype(BF16), jnp.where(own, glo, 0.0).astype(BF16)], axis=1))
+            near = jnp.dot(xs[group_rows(i), :], w_shift[...], preferred_element_type=F32)
+            near = near + jnp.dot(jnp.concatenate(parts, axis=0), w_ghost[...], preferred_element_type=F32)
+            for j in range(GROUP):
+                l = i * GROUP + j
+                k0, ke, kw, kn, ks = c0[l], ce[l], cw[l], cn[l], cs[l]
+                for t in range(2):
+                    k = 2 * j + t
+                    rows = near[k * OY:(k + 1) * OY]
+                    y = k0 * now[l, t, TOP:TOP + OY, :] + ke * rows[:, :LN] + kw * rows[:, LN:]
+                    y = y + kn * now[l, t, TOP + 1:TOP + 1 + OY, :] + ks * now[l, t, TOP - 1:TOP - 1 + OY, :]
+                    later[l, t, TOP:TOP + OY, :] = y
+                    if s < ADV - 1:
+                        p = 2 * l + t
+                        keep(p, y)
+                        rsend[s + 1, 0, pl.ds(p, 1), :] = y[OY - 1:OY]
+                        rsend[s + 1, 1, pl.ds(p, 1), :] = y[0:1]
+            return carry
+
+        lax.fori_loop(0, LO // GROUP, substep, 0)
         if s < ADV - 1:
-            csend[s + 1, 0] = acc
+            csend[s + 1, 0] = lax.fori_loop(0, LO // GROUP, edge_columns, zero48)
             for k in range(2):
                 rsend[s + 1, k, PL:64, :] = jnp.zeros((64 - PL, LN), F32)
             send_edges(s + 1)
+            exchange_part(s + 1)
 
     loads[9].wait()
 
@@ -318,9 +404,9 @@
         elim_r[l + 1] = r
         elim_z[0, l + 1] = yt * inv
         elim_z[1, l + 1] = ys * inv
-        return (1.0 + k * (1.0 - r), v[0, l, TOP:TOP + OY, :] + r * yt, v[0, LO + l, TOP:TOP + OY, :] + r * ys)
-
-    start = (jnp.ones((OY, LN), F32), v[0, LO - 1, TOP:TOP + OY, :], v[0, PL - 1, TOP:TOP + OY, :])
+        return (1.0 + k * (1.0 - r), va[l, 0, TOP:TOP + OY, :] + r * yt, va[l, 1, TOP:TOP + OY, :] + r * ys)
+
+    start = (jnp.ones((OY, LN), F32), va[LO - 1, 0, TOP:TOP + OY, :], va[LO - 1, 1, TOP:TOP + OY, :])
     e, yt, ys = lax.fori_loop(0, LO - 1, up, start)
     inv = 1.0 / e
     top_y[0], top_y[1], top_y[2] = yt, ys, inv
@@ -343,36 +429,29 @@
     air_z[0] = ya
     air_r[0] = inv_a
 
-    def exchange_wait(snd_buf, rcv_buf, k):
-        return pltpu.make_async_remote_copy(
-            src_ref=snd_buf.at[pl.ds(0, DEV - 1)], dst_ref=rcv_buf.at[pl.ds(0, DEV - 1)],
-            send_sem=a_sem.at[2 * k], recv_sem=a_sem.at[2 * k + 1], device_id=(east, gy), device_id_type=MESH)
-
-    exchange_wait(send1, recv1, 0).wait_recv()
-
     def apply_tiles(tile_ref, c, h):
-        total = jnp.zeros((NF, B, LN), F32)
+        out = jnp.zeros((NF, B, LN), F32)
         for a in range(B):
             w = tile_ref[c, a * B:(a + 1) * B, h * LN:(h + 1) * LN]
-            total = total + w[None] * xt[:, a:a + 1, :]
-        return total.reshape(NF * B, LN)
-
-    def spread(c, carry):
+            out = out + w[None] * xt[:, a:a + 1, :]
+        return out.reshape(NF * B, LN)
+
+    total[...] = jnp.zeros_like(total)
+
+    def spread(i, carry):
+        c = await_chunk(0, send1, recv1, i)
+        parts = []
         for h in range(2):
             xt[...] = recv1[pl.ds(c * 16 + h * 8, 8)].reshape(LN, LN).T.reshape(NF, B, LN)
-            hi, lo = split(apply_tiles(g1, c, h))
-            sp[2 * c + h, 0:LN, :] = hi
-            sp[2 * c + h, LN:, :] = lo
+            parts.append(jnp.concatenate(split(apply_tiles(g1, c, h)), axis=0))
+        total[...] += jnp.dot(
+            jnp.concatenate(parts, axis=1), oh_ht[pl.ds(2 * c, 2)].reshape(CW, 256), preferred_element_type=F32)
         return carry
 
     lax.fori_loop(0, CHUNKS, spread, 0)
 
-    def collect(g, total):
-        return total + lax.dot_general(
-            oh_h[g, 0:192, :], sp[g], (((1,), (1,)), ((), ())), preferred_element_type=F32)
-
-    both = lax.fori_loop(0, 16, collect, jnp.zeros((192, 256), F32))
-    landed = both[:, :LN] + both[:, LN:]
+    both = total[0:LN, :] + total[LN:, :]
+    landed = jnp.concatenate([both[:, :LN].T, both[:, LN:].T], axis=0)
     groups = [landed[q * OY:(q + 1) * OY] for q in range(4)]
     force = [blocks_to_field(groups, f) for f in range(NF)]
 
@@ -390,28 +469,20 @@
     st[...] = jnp.concatenate([lhi, llo], axis=0)
 
     def push(i, carry):
-        c = lax.rem(gx + 1 + i, GX)
+        c = chunk_order(i)
         for h in range(2):
             g = 2 * c + h
             two = jnp.dot(st[...], oh_h[g], preferred_element_type=F32)
             xt[...] = (two[:LN] + two[LN:]).reshape(NF, B, LN)
             send2[pl.ds(g * 8, 8)] = apply_tiles(g2, c, h).T.reshape(8, CAP, LN)
 
-        def out(j, carry2):
-            py = lax.rem(gy + j, GY)
-            copy = pltpu.make_async_remote_copy(
-                src_ref=send2.at[c * GY + py], dst_ref=recv2.at[me], send_sem=a_sem.at[2], recv_sem=a_sem.at[3],
-                device_id=(c, py), device_id_type=MESH)
-            copy.start()
-            return carry2
-
         @pl.when(i < GX - 1)
         def _():
-            lax.fori_loop(0, GY, out, 0)
+            send_chunk(1, send2, recv2, c, 0)
 
         @pl.when(i == GX - 1)
         def _():
-            lax.fori_loop(1, GY, out, 0)
+            send_chunk(1, send2, recv2, c, 1)
 
         return carry
 
@@ -434,13 +505,15 @@
     store = pltpu.make_async_copy(x_out, out_tr, out_sem)
     store.start()
 
-    exchange_wait(send2, recv2, 1).wait_recv()
-
-    def gather(g, total):
-        hi, lo = split(recv2[pl.ds(g * 8, 8)].reshape(LN, LN))
-        return total + jnp.dot(oh_b[g], jnp.concatenate([hi, lo], axis=1), preferred_element_type=F32)
-
-    both = lax.fori_loop(0, 16, gather, jnp.zeros((64, 256), F32))
+    def gather(i, carry):
+        c = await_chunk(1, send2, recv2, i)
+        for h in range(2):
+            g = 2 * c + h
+            hi, lo = split(recv2[pl.ds(g * 8, 8)].reshape(LN, LN))
+            carry = carry + jnp.dot(oh_b[g], jnp.concatenate([hi, lo], axis=1), preferred_element_type=F32)
+        return carry
+
+    both = lax.fori_loop(0, GX, gather, jnp.zeros((64, 256), F32))
     landed = both[:, :LN] + both[:, LN:]
     groups = [landed[q * AY:(q + 1) * AY] for q in range(4)]
     fields = [blocks_to_field(groups, f) for f in range(NF)]
@@ -453,11 +526,24 @@
         x = air_z[l] + air_r[l] * x
         out_air[l] = x
 
-    for s in range(ADV):
-        pass
-    exchange_wait(send1, recv1, 0).wait_send()
-    exchange_wait(send2, recv2, 1).wait_send()
+    exchange_wait(0, send1, recv1, gx, DEV - 1).wait_send()
+    exchange_wait(1, send2, recv2, gx, DEV - 1).wait_send()
     store.wait()
+
+
+def hand_on(tr, air, sf, out_tr, out_air, out_sf, tr_v, air_v, sf_v, sem_in, sem_out):
+    step = PL // PARTS
+    parts = [pl.ds(i * step, step) for i in range(PARTS)]
+    trios = [(tr.at[p], tr_v.at[p], out_tr.at[p]) for p in parts] + [(air, air_v, out_air), (sf, sf_v, out_sf)]
+    ins = [pltpu.make_async_copy(a, b, sem_in.at[i]) for i, (a, b, _) in enumerate(trios)]
+    outs = [pltpu.make_async_copy(b, c, sem_out.at[i]) for i, (_, b, c) in enumerate(trios)]
+    for copy in ins:
+        copy.start()
+    for copy, back in zip(ins, outs):
+        copy.wait()
+        back.start()
+    for back in outs:
+        back.wait()
 
 
 def shards(
@@ -468,20 +554,22 @@
     vm = pl.BlockSpec(memory_space=pltpu.VMEM)
     V = pltpu.VMEM
     scratch = [
-        V((2, PL, 64, LN), F32), V((LO, OY, LN), F32), V((LO, OY, LN), F32), V((LO - 1, OY, LN), F32),
+        V((LO, 2, 64, LN), F32), V((LO, 2, 64, LN), F32), V((PL * OY, 256), BF16), V((256, 256), BF16), V((256, 256), BF16),
+        V((256, LN), BF16), V((LO, OY, LN), F32), V((LO, OY, LN), F32), V((LO - 1, OY, LN), F32),
         V((OY, LN), jnp.int32), V((64, LN), F32), V((LA, AY, LN), F32), V((LA, AY, LN), F32), V((NF, AY, LN), F32),
-        V((64, 1024), F32), V((DEV, CAP), jnp.int32), V((DEV, CAP), jnp.int32), V((DEV, CAP), jnp.int32),
+        V((64, 1024), F32), V((CAP, DEV), jnp.int32), V((CAP, DEV), jnp.int32), V((CAP, DEV), jnp.int32),
         V((3, 16, LN), F32), V((2, 1024, LN), F32), V((2, 1024, LN), BF16),
-        V((16, LN, LN), BF16), V((16, 256, LN), BF16), V((16, 64, LN), BF16),
+        V((16, LN, LN), BF16), V((16, 256, LN), BF16), V((16, LN, 256), BF16),
+        V((16, 64, LN), BF16),
         V((CHUNKS, 1024, CW), F32), V((CHUNKS, 1024, CW), F32),
         V((DEV, CAP, LN), F32), V((DEV, CAP, LN), F32), V((DEV, CAP, LN), F32), V((DEV, CAP, LN), F32),
-        V((NF, B, LN), F32), V((16, 256, LN), BF16), V((256, 256), BF16),
+        V((NF, B, LN), F32), V((256, 256), F32), V((256, 256), BF16),
         V((ADV, 2, 96, LN), F32), V((ADV, 2, 96, LN), F32), V((ADV, 2, OY, LN), F32), V((ADV, 2, 2, OY, LN), F32),
         V((LO, OY, LN), F32), V((LO, OY, LN), F32), V((LO, OY, LN), F32), V((LO, OY, LN), F32), V((LO, OY, LN), F32),
         V((LO, OY, LN), F32), V((2, LO, OY, LN), F32), V((3, OY, LN), F32), V((LA, AY, LN), F32), V((LA, AY, LN), F32),
         V((PL, OY, LN), F32),
-        pltpu.SemaphoreType.DMA((12,)), pltpu.SemaphoreType.DMA, pltpu.SemaphoreType.DMA((ADV, 4)),
-        pltpu.SemaphoreType.DMA((ADV, 4)), pltpu.SemaphoreType.DMA((4,)),
+        pltpu.SemaphoreType.DMA((13,)), pltpu.SemaphoreType.DMA, pltpu.SemaphoreType.DMA((ADV, 4)),
+        pltpu.SemaphoreType.DMA((ADV, 4)), pltpu.SemaphoreType.DMA((2,)), pltpu.SemaphoreType.DMA((2, GX)),
     ]
     out_tr, out_air, out_sf = pl.pallas_call(
         kernel,
@@ -494,12 +582,28 @@
         out_specs=(anyspace, vm, vm),
         scratch_shapes=scratch,
         compiler_params=pltpu.CompilerParams(
-            collective_id=0, has_side_effects=True, vmem_limit_bytes=56 * 1024 * 1024),
+            collective_id=0, has_side_effects=True, vmem_limit_bytes=60 * 1024 * 1024),
         name="coupling_step",
     )(
-        tracers.reshape(PL, OY, LN), east_flow, north_flow, ocean_kappa, land_sea, air_temp, air_kappa, air_fluxes,
-        weight_tiles, tile_index, send_blocks, receive_blocks,
+        tracers, east_flow, north_flow, ocean_kappa, land_sea, air_temp, air_kappa, air_fluxes,
+        weight_tiles, *(jnp.swapaxes(x, 1, 2) for x in (tile_index, send_blocks, receive_blocks)),
     )
+    out_tr, out_air, out_sf = pl.pallas_call(
+        hand_on,
+        out_shape=(
+            jax.ShapeDtypeStruct((PL, OY, LN), F32),
+            jax.ShapeDtypeStruct((LA, AY, LN), F32),
+            jax.ShapeDtypeStruct((NF, AY, LN), F32),
+        ),
+        in_specs=[anyspace] * 3,
+        out_specs=[anyspace] * 3,
+        scratch_shapes=[
+            V((PL, OY, LN), F32), V((LA, AY, LN), F32), V((NF, AY, LN), F32),
+            pltpu.SemaphoreType.DMA((PARTS + 2,)), pltpu.SemaphoreType.DMA((PARTS + 2,)),
+        ],
+        compiler_params=pltpu.CompilerParams(vmem_limit_bytes=60 * 1024 * 1024),
+        name="hand_on",
+    )(out_tr, out_air, out_sf)
     return out_tr.reshape(2, LO, OY, LN), out_air, out_sf
 
 

time: 96 us -> 72.5 us (0.76)
  Pallas kernels: 86.9 us -> 71.7 us
  local copies, waits for them, and re-layouts: 8.15 us -> 0 us
    pallas_call x1, Pallas kernels: 86.9 us -> 69.4 us  [shards(): pl.pallas_call(kernel, out_shape=(jax.ShapeDtypeStruct((PL, OY, LN), F32)...]
    unnamed x10 -> x0, local copies, waits for them, and re-layouts: 8.15 us -> none
    pallas_call x0 -> x1, Pallas kernels: none -> 2.35 us  [shards(): pl.pallas_call(hand_on, out_shape=(jax.ShapeDtypeStruct((PL, OY, LN), F32...]
where the time goes in v2:
time: 72.5 us; the launch traced here: 72.4 us
  Pallas kernels  71.7 us (99%)
    pallas_call x1, Pallas kernels, shards(): pl.pallas_call(kernel, out_shape=(jax.ShapeDtypeStruct((PL, OY, LN), F32)...  69.4 us
    pallas_call x1, Pallas kernels, shards(): pl.pallas_call(hand_on, out_shape=(jax.ShapeDtypeStruct((PL, OY, LN), F32...  2.35 us

profile of v2, /device:TPU:1, one launch (start us, length us, event | category | flops | bytes accessed | tf_op | source)
XLA Modules:
  0.0 72.4 jit_solution(3450966805068705813)
XLA Ops:
  0.6 69.4 %coupling_step.1 = (f32[60,48,128]{2,1,0:T(8,128)}, f32[16,16,128]{2,1,0:T(8,128)}, f32[4,16,128]{2,1,0:T(8,128)}) custom-call(f32[2,30,48,128]{3,2,1,0:T(8,128)} %tr.1, f32[30,48,128]{2,1,0:T(8,128)} %ue.1, f32[30,48,128]{2,1,0:T(8,128)} %un.1, f32[29,48,128]{2,1,0:T(8,128)} %kap.1, s32[48,128]{1,0:T(8,128)} %land.1, f32[16,16,128]{2,1,0:T(8,128)} %atemp.1, ...), custom_call_target="tpu_custom_call" | custom-call | tf_op jit(solution)/shard_map/coupling_step/pallas_call | solution.py:574
  70.0 2.4 %hand_on.1 = (f32[60,48,128]{2,1,0:T(8,128)}, f32[16,16,128]{2,1,0:T(8,128)}, f32[4,16,128]{2,1,0:T(8,128)}) custom-call(f32[60,48,128]{2,1,0:T(8,128)} %get-tuple-element.9.tr, f32[16,16,128]{2,1,0:T(8,128)} %get-tuple-element.10.air, f32[4,16,128]{2,1,0:T(8,128)} %get-tuple-element.11.sf), custom_call_target="tpu_custom_call" | custom-call | tf_op jit(solution)/shard_map/hand_on/pallas_call | solution.py:591

commit v3 on v2

--- a/solution.py
+++ b/solution.py
@@ -16,9 +16,10 @@
 PL = 2 * LO
 TOP = 8
 CHUNKS, CW = 8, 256
-GROUP = 5
-SENDS = (3, 2, 2, 1)
+GROUP = 10
+SENDS = (3, 3, 2)
 PARTS = 6
+UNROLL = 2
 
 
 def iota(shape, dim):
@@ -33,7 +34,7 @@
 def fields_to_blocks(fields, q):
     lane = iota(fields[0].shape, 1) >> 5
     out = jnp.zeros_like(fields[0])
-    for f in range(NF):
+    for f in range(len(fields)):
         moved = pltpu.roll(fields[f], ((f - q) * B) % LN, 1) if f != q else fields[f]
         out = jnp.where(lane == f, moved, out)
     return out
@@ -49,18 +50,33 @@
 
 
 def slot_rows(idx):
-    spread = (iota((CAP, LN), 1) & (CAP - 1)) == iota((CAP, LN), 0)
+    lane = iota((CAP, LN), 1)
+    spread = 2 * (lane & 7) + (lane >> 6) == iota((CAP, LN), 0)
     tiled = jnp.dot(idx.astype(F32).T.astype(BF16), spread.astype(F32).astype(BF16), preferred_element_type=F32)
-    own = (iota((DEV, LN), 1) >> 4) == (iota((DEV, LN), 0) & 7)
+    own = ((iota((DEV, LN), 1) >> 3) & 7) == (iota((DEV, LN), 0) & 7)
     return jnp.sum(jnp.where(own, tiled, 0.0).reshape(16, 8, LN), axis=1)
+
+
+def mix_halves(a, b):
+    low = iota(a.shape, 1) < 64
+    return jnp.where(low, a, pltpu.roll(b, 64, 1)), jnp.where(low, pltpu.roll(a, 64, 1), b)
+
+
+def pack(a, b):
+    return jnp.concatenate(mix_halves(a, b), axis=0).T
+
+
+def unpack(rows):
+    turned = rows.T
+    return mix_halves(turned[:64], turned[64:])
 
 
 def kernel(
     tr, ue, un, kap, land, atemp, akap, aflux, wts, tix, sbl, rbl,
     out_tr, out_air, out_sf,
-    va, vb, xs, w_shift, w_ghost, w_edge, u, n, kv, land_v, sea_p, at_v, ak_v, af_v, w_v, ti_v, sb_v, rb_v,
+    va, vb, xs, w_shift, w_edge, u, n, kv, land_v, sea_p, at_v, ak_v, af_v, w_v, ti_v, sb_v, rb_v,
     rows3, w2t, w2p, oh_t, oh_h, oh_ht, oh_b, g1, g2,
-    send1, recv1, send2, recv2, xt, total, st,
+    box_out, box_in, xt, total, st,
     rsend, rrecv, csend, crecv,
     c0, ce, cw, cn, cs, elim_r, elim_z, top_y, air_r, air_z, x_out,
     in_sem, out_sem, hs_sem, hr_sem, as_sem, ar_sem,
@@ -99,18 +115,21 @@
     air = [af_v[f] for f in range(NF)]
     blocks = jnp.concatenate([fields_to_blocks(air, q) for q in range(4)], axis=0)
     bhi, blo = split(blocks)
-    blocks2 = jnp.concatenate([bhi, blo], axis=0)
+    blocks2 = jnp.concatenate([bhi.astype(F32), blo.astype(F32)], axis=0).T.astype(BF16)
     sub128 = iota((LN, LN), 0)
 
-    def pick(g, carry):
-        row = rows3[1, pl.ds(g, 1), :]
-        hot = jnp.where((sub128 & 63).astype(F32) == row, 1.0, 0.0)
-        oh_b[g] = hot[:64].astype(BF16)
-        picked = jnp.dot(hot.T.astype(BF16), blocks2, preferred_element_type=F32)
-        send1[pl.ds(g * 8, 8)] = picked.reshape(8, CAP, LN)
+    def pick(c, carry):
+        hot = [jnp.where((sub128 & 63).astype(F32) == rows3[1, pl.ds(2 * c + h, 1), :], 1.0, 0.0) for h in range(2)]
+        oh_b[c] = jnp.concatenate(mix_halves(hot[0][:64], hot[1][:64]), axis=0).astype(BF16)
+        picked = jnp.dot(blocks2, jnp.concatenate(hot, axis=1).astype(BF16), preferred_element_type=F32)
+        a, b = picked[:, :LN], picked[:, LN:]
+        box_out[0, pl.ds(c * 16, 16)] = pack(a[64:], b[64:]).reshape(16, 8, LN)
+        box_out[1, pl.ds(c * 16, 16)] = pack(a[:64], b[:64]).reshape(16, 8, LN)
         return carry
 
-    lax.fori_loop(0, 16, pick, 0)
+    lax.fori_loop(0, CHUNKS, pick, 0)
+    box_in[0, me] = box_out[0, me]
+    box_in[1, me] = box_out[1, me]
 
     for i in (2, 3, 4, 5, 12):
         loads[i].wait()
@@ -120,9 +139,9 @@
     src, dst = iota((256, 256), 0) & (LN - 1), iota((256, 256), 1)
     to_east = (src == dst + 1) & (dst < LN - 1)
     to_west = (src == dst - 1 - LN) & (dst > LN)
-    w_shift[...] = jnp.where(to_east | to_west, 1.0, 0.0).astype(BF16)
+    w_shift[0:256, :] = jnp.where(to_east | to_west, 1.0, 0.0).astype(BF16)
     even = (src & 1) == 0
-    w_ghost[...] = jnp.where((even & (dst == LN - 1)) | ((src & 1 == 1) & (dst == LN)), 1.0, 0.0).astype(BF16)
+    w_shift[256:512, :] = jnp.where((even & (dst == LN - 1)) | ((src & 1 == 1) & (dst == LN)), 1.0, 0.0).astype(BF16)
     src, dst = iota((256, LN), 0) & (LN - 1), iota((256, LN), 1)
     even = (dst & 1) == 0
     w_edge[...] = jnp.where((even & (src == LN - 1)) | ((dst & 1 == 1) & (src == 0)), 1.0, 0.0).astype(BF16)
@@ -133,10 +152,12 @@
     def group_rows(i):
         return pl.ds(pl.multiple_of(i * (2 * GROUP * OY), 2 * GROUP * OY), 2 * GROUP * OY)
 
-    def edge_columns(i, acc):
-        found = jnp.dot(xs[group_rows(i), :], w_edge[...], preferred_element_type=F32)
-        for k in range(2 * GROUP):
-            acc = jnp.where((lane48 >> 1) == i * 2 * GROUP + k, found[k * OY:(k + 1) * OY], acc)
+    def edge_columns():
+        acc = jnp.zeros((OY, LN), F32)
+        for i in range(LO // GROUP):
+            found = jnp.dot(xs[group_rows(i), :], w_edge[...], preferred_element_type=F32)
+            for k in range(2 * GROUP):
+                acc = jnp.where((lane48 >> 1) == i * 2 * GROUP + k, found[k * OY:(k + 1) * OY], acc)
         return acc
 
     def first_edges(i, accu):
@@ -154,7 +175,7 @@
 
     zero48 = jnp.zeros((OY, LN), F32)
     accu = lax.fori_loop(0, LO // GROUP, first_edges, zero48)
-    acc = lax.fori_loop(0, LO // GROUP, edge_columns, zero48)
+    acc = edge_columns()
     acc = jnp.where((lane48 >> 1) == PL, pltpu.roll(sea, 2 * PL + 1, 1), acc)
     csend[0, 0] = acc
     csend[0, 1] = accu
@@ -223,54 +244,48 @@
 
     send_edges(0)
 
-    def exchange_copy(k, snd_buf, rcv_buf, px, py):
+    def send_chunk(k, c, start):
+        def out(j, carry):
+            py = lax.rem(gy + j, GY)
+            pltpu.make_async_remote_copy(
+                src_ref=box_out.at[k, c * GY + py], dst_ref=box_in.at[k, me], send_sem=as_sem.at[k],
+                recv_sem=ar_sem.at[k, gx], device_id=(c, py), device_id_type=MESH).start()
+            return carry
+
+        lax.fori_loop(start, GY, out, 0)
+
+    def exchange_wait(k, c, blocks):
         return pltpu.make_async_remote_copy(
-            src_ref=snd_buf.at[px * GY + py], dst_ref=rcv_buf.at[me], send_sem=as_sem.at[k], recv_sem=ar_sem.at[k, gx],
-            device_id=(px, py), device_id_type=MESH)
-
-    def send_chunk(k, snd_buf, rcv_buf, c, start):
-        def out(j, carry):
-            exchange_copy(k, snd_buf, rcv_buf, c, lax.rem(gy + j, GY)).start()
-            return carry
-
-        lax.fori_loop(start, GY, out, 0)
-
-    def exchange_wait(k, snd_buf, rcv_buf, c, blocks):
-        return pltpu.make_async_remote_copy(
-            src_ref=snd_buf.at[pl.ds(0, blocks)], dst_ref=rcv_buf.at[pl.ds(0, blocks)],
+            src_ref=box_out.at[k, pl.ds(0, blocks)], dst_ref=box_in.at[k, pl.ds(0, blocks)],
             send_sem=as_sem.at[k], recv_sem=ar_sem.at[k, c], device_id=(east, gy), device_id_type=MESH)
 
     def chunk_order(i):
         return lax.rem(gx + 1 + i, GX)
 
-    def arrival_order(i):
-        return lax.rem(gx + GX - 1 - i, GX)
-
-    def await_chunk(k, snd_buf, rcv_buf, i):
-        c = arrival_order(i)
+    def await_chunk(k, i):
+        c = lax.rem(gx + GX - 1 - i, GX)
 
         @pl.when(i < GX - 1)
         def _():
-            exchange_wait(k, snd_buf, rcv_buf, c, GY).wait_recv()
+            exchange_wait(k, c, GY).wait_recv()
 
         @pl.when(i == GX - 1)
         def _():
-            exchange_wait(k, snd_buf, rcv_buf, c, GY - 1).wait_recv()
+            exchange_wait(k, c, GY - 1).wait_recv()
 
         return c
 
-    def exchange_out(i, carry):
-        send_chunk(0, send1, recv1, chunk_order(i), 0)
-        return carry
-
-    def exchange_part(s):
-        begin, end = sum(SENDS[:s]), sum(SENDS[:s + 1])
-        lax.fori_loop(begin, min(end, GX - 1), exchange_out, 0)
-        if end == GX and SENDS[s] > 0:
-            send_chunk(0, send1, recv1, gx, 1)
-
-    exchange_part(0)
-    recv1[me] = send1[me]
+    def exchange_part(k, begin, end):
+        def out(i, carry):
+            send_chunk(k, chunk_order(i), 0)
+            return carry
+
+        if begin < min(end, GX - 1):
+            lax.fori_loop(begin, min(end, GX - 1), out, 0)
+        if begin < end == GX:
+            send_chunk(k, gx, 1)
+
+    exchange_part(0, 0, GX)
 
     for i in (6, 7, 8):
         loads[i].wait()
@@ -280,11 +295,10 @@
     for c in range(8):
         whi, wlo = split(w_v[:, c * LN:(c + 1) * LN])
         both = jnp.concatenate([whi.astype(F32), wlo.astype(F32)], axis=0)
-        w2t[0, c * LN:(c + 1) * LN, :] = both.T
+        w2t[c * LN:(c + 1) * LN, :] = both.T
+    w2p[0] = w2t[...].astype(BF16)
     for b in range(B):
-        w2t[1, b * B:(b + 1) * B, :] = w2t[0, pl.ds(b, B, stride=B), :]
-    w2p[0] = w2t[0].astype(BF16)
-    w2p[1] = w2t[1].astype(BF16)
+        w2p[1, b * B:(b + 1) * B, :] = w2t[pl.ds(b, B, stride=B), :].astype(BF16)
 
     def hots(g, carry):
         rt = rows3[0, pl.ds(g, 1), :]
@@ -298,13 +312,15 @@
 
     lax.fori_loop(0, 16, hots, 0)
 
-    def tiles(c, carry):
-        hot = jnp.concatenate([oh_t[2 * c], oh_t[2 * c + 1]], axis=1)
-        g1[c] = jnp.dot(w2p[0], hot, preferred_element_type=F32)
-        g2[c] = jnp.dot(w2p[1], hot, preferred_element_type=F32)
-        return carry
-
-    lax.fori_loop(0, 2, tiles, 0)
+    def tiles(which, out):
+        def one(c, carry):
+            hot = jnp.concatenate([oh_t[2 * c], oh_t[2 * c + 1]], axis=1)
+            out[c] = jnp.dot(w2p[which], hot, preferred_element_type=F32)
+            return carry
+
+        lax.fori_loop(0, CHUNKS, one, 0)
+
+    tiles(0, g1)
 
     await_edges(0)
 
@@ -343,9 +359,102 @@
 
     lax.fori_loop(0, LO // GROUP, faces, 0)
 
+    def apply_tiles(tile_ref, c, h, slot):
+        out = jnp.zeros((2, B, LN), F32)
+        for a in range(B):
+            w = tile_ref[c, a * B:(a + 1) * B, h * LN:(h + 1) * LN]
+            out = out + w[None] * xt[slot, :, a:a + 1, :]
+        return out.reshape(2 * B, LN)
+
+    def forcing(e):
+        total[...] = jnp.zeros_like(total)
+
+        def arrive(i, carry):
+            await_chunk(e, i)
+            return carry
+
+        lax.fori_loop(0, CHUNKS, arrive, 0)
+
+        def spread(i, carry):
+            for d in range(UNROLL):
+                c = i * UNROLL + d
+                for h, x in enumerate(unpack(box_in[e, pl.ds(c * 16, 16)].reshape(LN, LN))):
+                    xt[2 * d + h] = x.reshape(2, B, LN)
+            parts = []
+            for d in range(UNROLL):
+                c = i * UNROLL + d
+                for h in range(2):
+                    parts.append(jnp.concatenate(split(apply_tiles(g1, c, h, 2 * d + h)), axis=0))
+            total[...] += jnp.dot(
+                jnp.concatenate(parts, axis=1), oh_ht[pl.ds(2 * UNROLL * i, 2 * UNROLL)].reshape(UNROLL * CW, 256),
+                preferred_element_type=F32)
+            return carry
+
+        lax.fori_loop(0, CHUNKS // UNROLL, spread, 0)
+        both = jnp.concatenate([total[0:64, :] + total[64:, :], jnp.zeros((64, 256), F32)], axis=0)
+        landed = jnp.concatenate([both[:, :LN].T, both[:, LN:].T], axis=0)
+        groups = [landed[q * OY:(q + 1) * OY] for q in range(4)]
+        return [blocks_to_field(groups, f) for f in range(2)]
+
+    def lift(surf):
+        sblocks = jnp.concatenate([fields_to_blocks(surf, q) for q in range(4)] + [jnp.zeros((64, LN), F32)], axis=0)
+        lifted = jnp.concatenate([sblocks[:LN].T[:64], sblocks[LN:].T[:64]], axis=1)
+        st[...] = jnp.concatenate(split(lifted), axis=0)
+
+    def send_terms(e):
+        k = 2 + e
+
+        def push(i, carry):
+            chunks = [chunk_order(i * UNROLL + d) for d in range(UNROLL)]
+            for d, c in enumerate(chunks):
+                for h in range(2):
+                    two = jnp.dot(st[...], oh_h[2 * c + h], preferred_element_type=F32)
+                    xt[2 * d + h] = (two[:64] + two[64:]).reshape(2, B, LN)
+            for d, c in enumerate(chunks):
+                parts = [apply_tiles(g2, c, h, 2 * d + h) for h in range(2)]
+                box_out[k, pl.ds(c * 16, 16)] = pack(*parts).reshape(16, 8, LN)
+            for d, c in enumerate(chunks):
+                if d < UNROLL - 1:
+                    send_chunk(k, c, 0)
+                    continue
+
+                @pl.when(i < GX // UNROLL - 1)
+                def _():
+                    send_chunk(k, c, 0)
+
+                @pl.when(i == GX // UNROLL - 1)
+                def _():
+                    send_chunk(k, c, 1)
+
+            return carry
+
+        lax.fori_loop(0, GX // UNROLL, push, 0)
+        box_in[k, me] = box_out[k, me]
+
+    def gather(e):
+        def add(i, carry):
+            c = await_chunk(2 + e, i)
+            rows = box_in[2 + e, pl.ds(c * 16, 16)].reshape(LN, LN)
+            return carry + jnp.dot(oh_b[c], jnp.concatenate(split(rows), axis=1), preferred_element_type=F32)
+
+        both = lax.fori_loop(0, GX, add, jnp.zeros((LN, 256), F32))
+        both = both[:, :LN] + both[:, LN:]
+        landed = both[:64] + pltpu.roll(both[64:], 64, 1)
+        groups = [landed[q * AY:(q + 1) * AY] for q in range(4)]
+        return [blocks_to_field(groups, f) for f in range(2)]
+
+    def before_wait(s):
+        if s == 1:
+            tiles(1, g2)
+        if s == 2:
+            f2, f3 = forcing(0)
+            lift([sea * (u[0] + 0.1 * jnp.tanh(f2)), sea * (n[0] + 0.1 * jnp.tanh(f3))])
+        if s == 3:
+            send_terms(0)
+
     for s in range(ADV):
         if s > 0:
-            lax.fori_loop(2 * s, 2 * s + 2, tiles, 0)
+            before_wait(s)
             await_edges(s)
         gh = ghosts(s)
         now, later = (va, vb) if s % 2 == 0 else (vb, va)
@@ -367,8 +476,9 @@
                 own = (lane48 >> 1) == i * 2 * GROUP + k
                 parts.append(jnp.concatenate(
                     [jnp.where(own, ghi, 0.0).astype(BF16), jnp.where(own, glo, 0.0).astype(BF16)], axis=1))
-            near = jnp.dot(xs[group_rows(i), :], w_shift[...], preferred_element_type=F32)
-            near = near + jnp.dot(jnp.concatenate(parts, axis=0), w_ghost[...], preferred_element_type=F32)
+            near = jnp.dot(
+                jnp.concatenate([xs[group_rows(i), :], jnp.concatenate(parts, axis=0)], axis=1), w_shift[...],
+                preferred_element_type=F32)
             for j in range(GROUP):
                 l = i * GROUP + j
                 k0, ke, kw, kn, ks = c0[l], ce[l], cw[l], cn[l], cs[l]
@@ -387,11 +497,11 @@
 
         lax.fori_loop(0, LO // GROUP, substep, 0)
         if s < ADV - 1:
-            csend[s + 1, 0] = lax.fori_loop(0, LO // GROUP, edge_columns, zero48)
+            csend[s + 1, 0] = edge_columns()
             for k in range(2):
                 rsend[s + 1, k, PL:64, :] = jnp.zeros((64 - PL, LN), F32)
             send_edges(s + 1)
-            exchange_part(s + 1)
+            exchange_part(1, sum(SENDS[:s]), sum(SENDS[:s + 1]))
 
     loads[9].wait()
 
@@ -429,65 +539,11 @@
     air_z[0] = ya
     air_r[0] = inv_a
 
-    def apply_tiles(tile_ref, c, h):
-        out = jnp.zeros((NF, B, LN), F32)
-        for a in range(B):
-            w = tile_ref[c, a * B:(a + 1) * B, h * LN:(h + 1) * LN]
-            out = out + w[None] * xt[:, a:a + 1, :]
-        return out.reshape(NF * B, LN)
-
-    total[...] = jnp.zeros_like(total)
-
-    def spread(i, carry):
-        c = await_chunk(0, send1, recv1, i)
-        parts = []
-        for h in range(2):
-            xt[...] = recv1[pl.ds(c * 16 + h * 8, 8)].reshape(LN, LN).T.reshape(NF, B, LN)
-            parts.append(jnp.concatenate(split(apply_tiles(g1, c, h)), axis=0))
-        total[...] += jnp.dot(
-            jnp.concatenate(parts, axis=1), oh_ht[pl.ds(2 * c, 2)].reshape(CW, 256), preferred_element_type=F32)
-        return carry
-
-    lax.fori_loop(0, CHUNKS, spread, 0)
-
-    both = total[0:LN, :] + total[LN:, :]
-    landed = jnp.concatenate([both[:, :LN].T, both[:, LN:].T], axis=0)
-    groups = [landed[q * OY:(q + 1) * OY] for q in range(4)]
-    force = [blocks_to_field(groups, f) for f in range(NF)]
-
-    xt0 = (top_y[0] + sea * force[0]) * top_y[2]
-    xs0 = (top_y[1] + sea * force[1]) * top_y[2]
-    surf = [
-        sea * xt0,
-        sea,
-        sea * (u[0] + 0.1 * jnp.tanh(force[2])),
-        sea * (n[0] + 0.1 * jnp.tanh(force[3])),
-    ]
-    sblocks = jnp.concatenate([fields_to_blocks(surf, q) for q in range(4)] + [jnp.zeros((64, LN), F32)], axis=0)
-    lifted = jnp.concatenate([sblocks[:LN].T, sblocks[LN:].T], axis=1)
-    lhi, llo = split(lifted)
-    st[...] = jnp.concatenate([lhi, llo], axis=0)
-
-    def push(i, carry):
-        c = chunk_order(i)
-        for h in range(2):
-            g = 2 * c + h
-            two = jnp.dot(st[...], oh_h[g], preferred_element_type=F32)
-            xt[...] = (two[:LN] + two[LN:]).reshape(NF, B, LN)
-            send2[pl.ds(g * 8, 8)] = apply_tiles(g2, c, h).T.reshape(8, CAP, LN)
-
-        @pl.when(i < GX - 1)
-        def _():
-            send_chunk(1, send2, recv2, c, 0)
-
-        @pl.when(i == GX - 1)
-        def _():
-            send_chunk(1, send2, recv2, c, 1)
-
-        return carry
-
-    lax.fori_loop(0, GX, push, 0)
-    recv2[me] = send2[me]
+    f0, f1 = forcing(1)
+    xt0 = (top_y[0] + sea * f0) * top_y[2]
+    xs0 = (top_y[1] + sea * f1) * top_y[2]
+    lift([sea * xt0, sea])
+    send_terms(1)
 
     x_out[0] = xt0
     x_out[LO] = xs0
@@ -505,18 +561,8 @@
     store = pltpu.make_async_copy(x_out, out_tr, out_sem)
     store.start()
 
-    def gather(i, carry):
-        c = await_chunk(1, send2, recv2, i)
-        for h in range(2):
-            g = 2 * c + h
-            hi, lo = split(recv2[pl.ds(g * 8, 8)].reshape(LN, LN))
-            carry = carry + jnp.dot(oh_b[g], jnp.concatenate([hi, lo], axis=1), preferred_element_type=F32)
-        return carry
-
-    both = lax.fori_loop(0, GX, gather, jnp.zeros((64, 256), F32))
-    landed = both[:, :LN] + both[:, LN:]
-    groups = [landed[q * AY:(q + 1) * AY] for q in range(4)]
-    fields = [blocks_to_field(groups, f) for f in range(NF)]
+    late = gather(0)
+    fields = gather(1) + late
     for f in range(NF):
         out_sf[f] = fields[f]
     ground = at_v[0] * (1.0 - fields[1]) + fields[0]
@@ -526,8 +572,8 @@
         x = air_z[l] + air_r[l] * x
         out_air[l] = x
 
-    exchange_wait(0, send1, recv1, gx, DEV - 1).wait_send()
-    exchange_wait(1, send2, recv2, gx, DEV - 1).wait_send()
+    for k in range(4):
+        exchange_wait(k, gx, DEV - 1).wait_send()
     store.wait()
 
 
@@ -554,22 +600,22 @@
     vm = pl.BlockSpec(memory_space=pltpu.VMEM)
     V = pltpu.VMEM
     scratch = [
-        V((LO, 2, 64, LN), F32), V((LO, 2, 64, LN), F32), V((PL * OY, 256), BF16), V((256, 256), BF16), V((256, 256), BF16),
+        V((LO, 2, 64, LN), F32), V((LO, 2, 64, LN), F32), V((PL * OY, 256), BF16), V((512, 256), BF16),
         V((256, LN), BF16), V((LO, OY, LN), F32), V((LO, OY, LN), F32), V((LO - 1, OY, LN), F32),
         V((OY, LN), jnp.int32), V((64, LN), F32), V((LA, AY, LN), F32), V((LA, AY, LN), F32), V((NF, AY, LN), F32),
         V((64, 1024), F32), V((CAP, DEV), jnp.int32), V((CAP, DEV), jnp.int32), V((CAP, DEV), jnp.int32),
-        V((3, 16, LN), F32), V((2, 1024, LN), F32), V((2, 1024, LN), BF16),
+        V((3, 16, LN), F32), V((1024, LN), F32), V((2, 1024, LN), BF16),
         V((16, LN, LN), BF16), V((16, 256, LN), BF16), V((16, LN, 256), BF16),
-        V((16, 64, LN), BF16),
+        V((CHUNKS, LN, LN), BF16),
         V((CHUNKS, 1024, CW), F32), V((CHUNKS, 1024, CW), F32),
-        V((DEV, CAP, LN), F32), V((DEV, CAP, LN), F32), V((DEV, CAP, LN), F32), V((DEV, CAP, LN), F32),
-        V((NF, B, LN), F32), V((256, 256), F32), V((256, 256), BF16),
+        V((4, DEV, 8, LN), F32), V((4, DEV, 8, LN), F32),
+        V((2 * UNROLL, 2, B, LN), F32), V((LN, 256), F32), V((LN, 256), BF16),
         V((ADV, 2, 96, LN), F32), V((ADV, 2, 96, LN), F32), V((ADV, 2, OY, LN), F32), V((ADV, 2, 2, OY, LN), F32),
         V((LO, OY, LN), F32), V((LO, OY, LN), F32), V((LO, OY, LN), F32), V((LO, OY, LN), F32), V((LO, OY, LN), F32),
         V((LO, OY, LN), F32), V((2, LO, OY, LN), F32), V((3, OY, LN), F32), V((LA, AY, LN), F32), V((LA, AY, LN), F32),
         V((PL, OY, LN), F32),
         pltpu.SemaphoreType.DMA((13,)), pltpu.SemaphoreType.DMA, pltpu.SemaphoreType.DMA((ADV, 4)),
-        pltpu.SemaphoreType.DMA((ADV, 4)), pltpu.SemaphoreType.DMA((2,)), pltpu.SemaphoreType.DMA((2, GX)),
+        pltpu.SemaphoreType.DMA((ADV, 4)), pltpu.SemaphoreType.DMA((4,)), pltpu.SemaphoreType.DMA((4, GX)),
     ]
     out_tr, out_air, out_sf = pl.pallas_call(
         kernel,

time: 72.5 us -> 62.4 us (0.86)
  Pallas kernels: 71.7 us -> 61.6 us
    pallas_call x1, Pallas kernels: 69.4 us -> 59.3 us  [shards(): pl.pallas_call(kernel, out_shape=(jax.ShapeDtypeStruct((PL, OY, LN), F32)...]
where the time goes in v3:
time: 62.4 us; the launch traced here: 62.3 us
  Pallas kernels  61.6 us (99%)
  between operations  0.64 us (1%)
    pallas_call x1, Pallas kernels, shards(): pl.pallas_call(kernel, out_shape=(jax.ShapeDtypeStruct((PL, OY, LN), F32)...  59.3 us
    pallas_call x1, Pallas kernels, shards(): pl.pallas_call(hand_on, out_shape=(jax.ShapeDtypeStruct((PL, OY, LN), F32...  2.35 us

profile of v3, /device:TPU:1, one launch (start us, length us, event | category | flops | bytes accessed | tf_op | source)
XLA Modules:
  0.0 62.3 jit_solution(2996901105489457230)
XLA Ops:
  0.6 59.3 %coupling_step.1 = (f32[60,48,128]{2,1,0:T(8,128)}, f32[16,16,128]{2,1,0:T(8,128)}, f32[4,16,128]{2,1,0:T(8,128)}) custom-call(f32[2,30,48,128]{3,2,1,0:T(8,128)} %tr.1, f32[30,48,128]{2,1,0:T(8,128)} %ue.1, f32[30,48,128]{2,1,0:T(8,128)} %un.1, f32[29,48,128]{2,1,0:T(8,128)} %kap.1, s32[48,128]{1,0:T(8,128)} %land.1, f32[16,16,128]{2,1,0:T(8,128)} %atemp.1, ...), custom_call_target="tpu_custom_call" | custom-call | tf_op jit(solution)/shard_map/coupling_step/pallas_call | solution.py:620
  59.9 2.4 %hand_on.1 = (f32[60,48,128]{2,1,0:T(8,128)}, f32[16,16,128]{2,1,0:T(8,128)}, f32[4,16,128]{2,1,0:T(8,128)}) custom-call(f32[60,48,128]{2,1,0:T(8,128)} %get-tuple-element.9.tr, f32[16,16,128]{2,1,0:T(8,128)} %get-tuple-element.10.air, f32[4,16,128]{2,1,0:T(8,128)} %get-tuple-element.11.sf), custom_call_target="tpu_custom_call" | custom-call | tf_op jit(solution)/shard_map/hand_on/pallas_call | solution.py:637

commit v4 on v3

--- a/solution.py
+++ b/solution.py
@@ -17,7 +17,7 @@
 TOP = 8
 CHUNKS, CW = 8, 256
 GROUP = 10
-SENDS = (3, 3, 2)
+SENDS = (4, 4)
 PARTS = 6
 UNROLL = 2
 
@@ -76,7 +76,7 @@
     out_tr, out_air, out_sf,
     va, vb, xs, w_shift, w_edge, u, n, kv, land_v, sea_p, at_v, ak_v, af_v, w_v, ti_v, sb_v, rb_v,
     rows3, w2t, w2p, oh_t, oh_h, oh_ht, oh_b, g1, g2,
-    box_out, box_in, xt, total, st,
+    box1_out, box1_in, box_out, box_in, xt, total, st,
     rsend, rrecv, csend, crecv,
     c0, ce, cw, cn, cs, elim_r, elim_z, top_y, air_r, air_z, x_out,
     in_sem, out_sem, hs_sem, hr_sem, as_sem, ar_sem,
@@ -96,13 +96,11 @@
 
     barrier = pltpu.get_barrier_semaphore()
 
-    def greet(i, carry):
+    columns = [lax.rem(gx + i, GX) for i in range(GX)]
+    rows = [lax.rem(gy + j, GY) for j in range(GY)]
+    for i in range(1, DEV):
         pl.semaphore_signal(
-            barrier, inc=1, device_id=(lax.rem(gx + lax.div(i, GY), GX), lax.rem(gy + lax.rem(i, GY), GY)),
-            device_id_type=MESH)
-        return carry
-
-    lax.fori_loop(1, DEV, greet, 0)
+            barrier, inc=1, device_id=(columns[i // GY], rows[i % GY]), device_id_type=MESH)
 
     lane48 = iota((OY, LN), 1)
     row48 = iota((OY, LN), 0)
@@ -123,13 +121,12 @@
         oh_b[c] = jnp.concatenate(mix_halves(hot[0][:64], hot[1][:64]), axis=0).astype(BF16)
         picked = jnp.dot(blocks2, jnp.concatenate(hot, axis=1).astype(BF16), preferred_element_type=F32)
         a, b = picked[:, :LN], picked[:, LN:]
-        box_out[0, pl.ds(c * 16, 16)] = pack(a[64:], b[64:]).reshape(16, 8, LN)
-        box_out[1, pl.ds(c * 16, 16)] = pack(a[:64], b[:64]).reshape(16, 8, LN)
+        box1_out[pl.ds(c * 16, 16), 0:8, :] = pack(a[64:], b[64:]).reshape(16, 8, LN)
+        box1_out[pl.ds(c * 16, 16), 8:16, :] = pack(a[:64], b[:64]).reshape(16, 8, LN)
         return carry
 
     lax.fori_loop(0, CHUNKS, pick, 0)
-    box_in[0, me] = box_out[0, me]
-    box_in[1, me] = box_out[1, me]
+    box1_in[me] = box1_out[me]
 
     for i in (2, 3, 4, 5, 12):
         loads[i].wait()
@@ -244,19 +241,18 @@
 
     send_edges(0)
 
+    outs = (box1_out, box_out.at[0], box_out.at[1])
+    ins = (box1_in, box_in.at[0], box_in.at[1])
+
     def send_chunk(k, c, start):
-        def out(j, carry):
-            py = lax.rem(gy + j, GY)
+        for py in rows[start:]:
             pltpu.make_async_remote_copy(
-                src_ref=box_out.at[k, c * GY + py], dst_ref=box_in.at[k, me], send_sem=as_sem.at[k],
+                src_ref=outs[k].at[c * GY + py], dst_ref=ins[k].at[me], send_sem=as_sem.at[k],
                 recv_sem=ar_sem.at[k, gx], device_id=(c, py), device_id_type=MESH).start()
-            return carry
-
-        lax.fori_loop(start, GY, out, 0)
 
     def exchange_wait(k, c, blocks):
         return pltpu.make_async_remote_copy(
-            src_ref=box_out.at[k, pl.ds(0, blocks)], dst_ref=box_in.at[k, pl.ds(0, blocks)],
+            src_ref=outs[k].at[pl.ds(0, blocks)], dst_ref=ins[k].at[pl.ds(0, blocks)],
             send_sem=as_sem.at[k], recv_sem=ar_sem.at[k, c], device_id=(east, gy), device_id_type=MESH)
 
     def chunk_order(i):
@@ -285,7 +281,7 @@
         if begin < end == GX:
             send_chunk(k, gx, 1)
 
-    exchange_part(0, 0, GX)
+    exchange_part(0, 0, SENDS[0])
 
     for i in (6, 7, 8):
         loads[i].wait()
@@ -359,18 +355,18 @@
 
     lax.fori_loop(0, LO // GROUP, faces, 0)
 
-    def apply_tiles(tile_ref, c, h, slot):
-        out = jnp.zeros((2, B, LN), F32)
+    def apply_tiles(tile_ref, c, h, slot, count):
+        out = jnp.zeros((count, B, LN), F32)
         for a in range(B):
             w = tile_ref[c, a * B:(a + 1) * B, h * LN:(h + 1) * LN]
-            out = out + w[None] * xt[slot, :, a:a + 1, :]
-        return out.reshape(2 * B, LN)
-
-    def forcing(e):
+            out = out + w[None] * xt[slot, 0:count, a:a + 1, :]
+        return out.reshape(count * B, LN)
+
+    def forcing():
         total[...] = jnp.zeros_like(total)
 
         def arrive(i, carry):
-            await_chunk(e, i)
+            await_chunk(0, i)
             return carry
 
         lax.fori_loop(0, CHUNKS, arrive, 0)
@@ -378,23 +374,25 @@
         def spread(i, carry):
             for d in range(UNROLL):
                 c = i * UNROLL + d
-                for h, x in enumerate(unpack(box_in[e, pl.ds(c * 16, 16)].reshape(LN, LN))):
-                    xt[2 * d + h] = x.reshape(2, B, LN)
+                for e in range(2):
+                    rows = box1_in[pl.ds(c * 16, 16), 8 * e:8 * e + 8, :].reshape(LN, LN)
+                    for h, x in enumerate(unpack(rows)):
+                        xt[2 * d + h, 2 * e:2 * e + 2] = x.reshape(2, B, LN)
             parts = []
             for d in range(UNROLL):
                 c = i * UNROLL + d
                 for h in range(2):
-                    parts.append(jnp.concatenate(split(apply_tiles(g1, c, h, 2 * d + h)), axis=0))
+                    parts.append(jnp.concatenate(split(apply_tiles(g1, c, h, 2 * d + h, NF)), axis=0))
             total[...] += jnp.dot(
                 jnp.concatenate(parts, axis=1), oh_ht[pl.ds(2 * UNROLL * i, 2 * UNROLL)].reshape(UNROLL * CW, 256),
                 preferred_element_type=F32)
             return carry
 
         lax.fori_loop(0, CHUNKS // UNROLL, spread, 0)
-        both = jnp.concatenate([total[0:64, :] + total[64:, :], jnp.zeros((64, 256), F32)], axis=0)
+        both = total[0:LN, :] + total[LN:, :]
         landed = jnp.concatenate([both[:, :LN].T, both[:, LN:].T], axis=0)
         groups = [landed[q * OY:(q + 1) * OY] for q in range(4)]
-        return [blocks_to_field(groups, f) for f in range(2)]
+        return [blocks_to_field(groups, f) for f in range(NF)]
 
     def lift(surf):
         sblocks = jnp.concatenate([fields_to_blocks(surf, q) for q in range(4)] + [jnp.zeros((64, LN), F32)], axis=0)
@@ -402,17 +400,17 @@
         st[...] = jnp.concatenate(split(lifted), axis=0)
 
     def send_terms(e):
-        k = 2 + e
+        k = 1 + e
 
         def push(i, carry):
             chunks = [chunk_order(i * UNROLL + d) for d in range(UNROLL)]
             for d, c in enumerate(chunks):
                 for h in range(2):
                     two = jnp.dot(st[...], oh_h[2 * c + h], preferred_element_type=F32)
-                    xt[2 * d + h] = (two[:64] + two[64:]).reshape(2, B, LN)
+                    xt[2 * d + h, 0:2] = (two[:64] + two[64:]).reshape(2, B, LN)
             for d, c in enumerate(chunks):
-                parts = [apply_tiles(g2, c, h, 2 * d + h) for h in range(2)]
-                box_out[k, pl.ds(c * 16, 16)] = pack(*parts).reshape(16, 8, LN)
+                parts = [apply_tiles(g2, c, h, 2 * d + h, 2) for h in range(2)]
+                box_out[e, pl.ds(c * 16, 16)] = pack(*parts).reshape(16, 8, LN)
             for d, c in enumerate(chunks):
                 if d < UNROLL - 1:
                     send_chunk(k, c, 0)
@@ -429,12 +427,12 @@
             return carry
 
         lax.fori_loop(0, GX // UNROLL, push, 0)
-        box_in[k, me] = box_out[k, me]
+        box_in[e, me] = box_out[e, me]
 
     def gather(e):
         def add(i, carry):
-            c = await_chunk(2 + e, i)
-            rows = box_in[2 + e, pl.ds(c * 16, 16)].reshape(LN, LN)
+            c = await_chunk(1 + e, i)
+            rows = box_in[e, pl.ds(c * 16, 16)].reshape(LN, LN)
             return carry + jnp.dot(oh_b[c], jnp.concatenate(split(rows), axis=1), preferred_element_type=F32)
 
         both = lax.fori_loop(0, GX, add, jnp.zeros((LN, 256), F32))
@@ -447,7 +445,8 @@
         if s == 1:
             tiles(1, g2)
         if s == 2:
-            f2, f3 = forcing(0)
+            f2, f3, f0, f1 = forcing()
+            top_y[3], top_y[4] = f0, f1
             lift([sea * (u[0] + 0.1 * jnp.tanh(f2)), sea * (n[0] + 0.1 * jnp.tanh(f3))])
         if s == 3:
             send_terms(0)
@@ -501,7 +500,8 @@
             for k in range(2):
                 rsend[s + 1, k, PL:64, :] = jnp.zeros((64 - PL, LN), F32)
             send_edges(s + 1)
-            exchange_part(1, sum(SENDS[:s]), sum(SENDS[:s + 1]))
+            if s + 1 < len(SENDS):
+                exchange_part(0, sum(SENDS[:s + 1]), sum(SENDS[:s + 2]))
 
     loads[9].wait()
 
@@ -539,9 +539,8 @@
     air_z[0] = ya
     air_r[0] = inv_a
 
-    f0, f1 = forcing(1)
-    xt0 = (top_y[0] + sea * f0) * top_y[2]
-    xs0 = (top_y[1] + sea * f1) * top_y[2]
+    xt0 = (top_y[0] + sea * top_y[3]) * top_y[2]
+    xs0 = (top_y[1] + sea * top_y[4]) * top_y[2]
     lift([sea * xt0, sea])
     send_terms(1)
 
@@ -572,7 +571,7 @@
         x = air_z[l] + air_r[l] * x
         out_air[l] = x
 
-    for k in range(4):
+    for k in range(3):
         exchange_wait(k, gx, DEV - 1).wait_send()
     store.wait()
 
@@ -608,14 +607,14 @@
         V((16, LN, LN), BF16), V((16, 256, LN), BF16), V((16, LN, 256), BF16),
         V((CHUNKS, LN, LN), BF16),
         V((CHUNKS, 1024, CW), F32), V((CHUNKS, 1024, CW), F32),
-        V((4, DEV, 8, LN), F32), V((4, DEV, 8, LN), F32),
-        V((2 * UNROLL, 2, B, LN), F32), V((LN, 256), F32), V((LN, 256), BF16),
+        V((DEV, 16, LN), F32), V((DEV, 16, LN), F32), V((2, DEV, 8, LN), F32), V((2, DEV, 8, LN), F32),
+        V((2 * UNROLL, NF, B, LN), F32), V((256, 256), F32), V((LN, 256), BF16),
         V((ADV, 2, 96, LN), F32), V((ADV, 2, 96, LN), F32), V((ADV, 2, OY, LN), F32), V((ADV, 2, 2, OY, LN), F32),
         V((LO, OY, LN), F32), V((LO, OY, LN), F32), V((LO, OY, LN), F32), V((LO, OY, LN), F32), V((LO, OY, LN), F32),
-        V((LO, OY, LN), F32), V((2, LO, OY, LN), F32), V((3, OY, LN), F32), V((LA, AY, LN), F32), V((LA, AY, LN), F32),
+        V((LO, OY, LN), F32), V((2, LO, OY, LN), F32), V((5, OY, LN), F32), V((LA, AY, LN), F32), V((LA, AY, LN), F32),
         V((PL, OY, LN), F32),
         pltpu.SemaphoreType.DMA((13,)), pltpu.SemaphoreType.DMA, pltpu.SemaphoreType.DMA((ADV, 4)),
-        pltpu.SemaphoreType.DMA((ADV, 4)), pltpu.SemaphoreType.DMA((4,)), pltpu.SemaphoreType.DMA((4, GX)),
+        pltpu.SemaphoreType.DMA((ADV, 4)), pltpu.SemaphoreType.DMA((3,)), pltpu.SemaphoreType.DMA((3, GX)),
     ]
     out_tr, out_air, out_sf = pl.pallas_call(
         kernel,

time: 62.4 us -> 60.1 us (0.963)
  Pallas kernels: 61.6 us -> 59.3 us
    pallas_call x1, Pallas kernels: 59.3 us -> 56.9 us  [shards(): pl.pallas_call(kernel, out_shape=(jax.ShapeDtypeStruct((PL, OY, LN), F32)...]
where the time goes in v4:
time: 60.1 us; the launch traced here: 59.9 us
  Pallas kernels  59.3 us (99%)
  between operations  0.64 us (1%)
    pallas_call x1, Pallas kernels, shards(): pl.pallas_call(kernel, out_shape=(jax.ShapeDtypeStruct((PL, OY, LN), F32)...  56.9 us
    pallas_call x1, Pallas kernels, shards(): pl.pallas_call(hand_on, out_shape=(jax.ShapeDtypeStruct((PL, OY, LN), F32...  2.35 us

profile of v4, /device:TPU:1, one launch (start us, length us, event | category | flops | bytes accessed | tf_op | source)
XLA Modules:
  0.0 59.9 jit_solution(15798773066666510247)
XLA Ops:
  0.6 56.9 %coupling_step.1 = (f32[60,48,128]{2,1,0:T(8,128)}, f32[16,16,128]{2,1,0:T(8,128)}, f32[4,16,128]{2,1,0:T(8,128)}) custom-call(f32[2,30,48,128]{3,2,1,0:T(8,128)} %tr.1, f32[30,48,128]{2,1,0:T(8,128)} %ue.1, f32[30,48,128]{2,1,0:T(8,128)} %un.1, f32[29,48,128]{2,1,0:T(8,128)} %kap.1, s32[48,128]{1,0:T(8,128)} %land.1, f32[16,16,128]{2,1,0:T(8,128)} %atemp.1, ...), custom_call_target="tpu_custom_call" | custom-call | tf_op jit(solution)/shard_map/coupling_step/pallas_call | solution.py:619
  57.6 2.4 %hand_on.1 = (f32[60,48,128]{2,1,0:T(8,128)}, f32[16,16,128]{2,1,0:T(8,128)}, f32[4,16,128]{2,1,0:T(8,128)}) custom-call(f32[60,48,128]{2,1,0:T(8,128)} %get-tuple-element.9.tr, f32[16,16,128]{2,1,0:T(8,128)} %get-tuple-element.10.air, f32[4,16,128]{2,1,0:T(8,128)} %get-tuple-element.11.sf), custom_call_target="tpu_custom_call" | custom-call | tf_op jit(solution)/shard_map/hand_on/pallas_call | solution.py:636

commit v5 on v4

--- a/solution.py
+++ b/solution.py
@@ -78,7 +78,7 @@
     rows3, w2t, w2p, oh_t, oh_h, oh_ht, oh_b, g1, g2,
     box1_out, box1_in, box_out, box_in, xt, total, st,
     rsend, rrecv, csend, crecv,
-    c0, ce, cw, cn, cs, elim_r, elim_z, top_y, air_r, air_z, x_out,
+    c0, ce, cw, cn, cs, elim_r, elim_i, elim_z, top_y, air_r, air_z, x_out,
     in_sem, out_sem, hs_sem, hr_sem, as_sem, ar_sem,
 ):
     gx = lax.axis_index("gx")
@@ -469,32 +469,34 @@
         lax.fori_loop(0, LO // GROUP, edges_in, 0)
         ghi, glo = (x.astype(F32) for x in split(gh))
 
-        def substep(i, carry, s=s, now=now, later=later, ghi=ghi, glo=glo):
-            parts = []
-            for k in range(2 * GROUP):
-                own = (lane48 >> 1) == i * 2 * GROUP + k
+        def substep(i, carry, s=s, now=now, later=later, ghi=ghi, glo=glo, tracers=(0, 1)):
+            planes = [(i * GROUP + j, t) for j in range(GROUP) for t in tracers]
+            parts, lines_here = [], []
+            for l, t in planes:
+                p = 2 * l + t
+                own = (lane48 >> 1) == p
                 parts.append(jnp.concatenate(
                     [jnp.where(own, ghi, 0.0).astype(BF16), jnp.where(own, glo, 0.0).astype(BF16)], axis=1))
+                lines_here.append(xs[pl.ds(pl.multiple_of(p * OY, OY), OY), :])
             near = jnp.dot(
-                jnp.concatenate([xs[group_rows(i), :], jnp.concatenate(parts, axis=0)], axis=1), w_shift[...],
-                preferred_element_type=F32)
-            for j in range(GROUP):
-                l = i * GROUP + j
-                k0, ke, kw, kn, ks = c0[l], ce[l], cw[l], cn[l], cs[l]
-                for t in range(2):
-                    k = 2 * j + t
-                    rows = near[k * OY:(k + 1) * OY]
-                    y = k0 * now[l, t, TOP:TOP + OY, :] + ke * rows[:, :LN] + kw * rows[:, LN:]
-                    y = y + kn * now[l, t, TOP + 1:TOP + 1 + OY, :] + ks * now[l, t, TOP - 1:TOP - 1 + OY, :]
-                    later[l, t, TOP:TOP + OY, :] = y
-                    if s < ADV - 1:
-                        p = 2 * l + t
-                        keep(p, y)
-                        rsend[s + 1, 0, pl.ds(p, 1), :] = y[OY - 1:OY]
-                        rsend[s + 1, 1, pl.ds(p, 1), :] = y[0:1]
+                jnp.concatenate([jnp.concatenate(lines_here, axis=0), jnp.concatenate(parts, axis=0)], axis=1),
+                w_shift[...], preferred_element_type=F32)
+            for k, (l, t) in enumerate(planes):
+                near_k = near[k * OY:(k + 1) * OY]
+                y = c0[l] * now[l, t, TOP:TOP + OY, :] + ce[l] * near_k[:, :LN] + cw[l] * near_k[:, LN:]
+                y = y + cn[l] * now[l, t, TOP + 1:TOP + 1 + OY, :] + cs[l] * now[l, t, TOP - 1:TOP - 1 + OY, :]
+                later[l, t, TOP:TOP + OY, :] = y
+                if s < ADV - 1:
+                    p = 2 * l + t
+                    keep(p, y)
+                    rsend[s + 1, 0, pl.ds(p, 1), :] = y[OY - 1:OY]
+                    rsend[s + 1, 1, pl.ds(p, 1), :] = y[0:1]
             return carry
 
-        lax.fori_loop(0, LO // GROUP, substep, 0)
+        if s < ADV - 1:
+            lax.fori_loop(0, LO // GROUP, substep, 0)
+        else:
+            lax.fori_loop(0, LO // GROUP, lambda i, carry, f=substep: f(i, carry, tracers=(0,)), 0)
         if s < ADV - 1:
             csend[s + 1, 0] = edge_columns()
             for k in range(2):
@@ -506,20 +508,18 @@
     loads[9].wait()
 
     def up(i, carry):
-        e, yt, ys = carry
+        e, yt = carry
         l = LO - 2 - i
         k = kv[l] * sea
         inv = 1.0 / (e + k)
         r = k * inv
         elim_r[l + 1] = r
+        elim_i[l + 1] = inv
         elim_z[0, l + 1] = yt * inv
-        elim_z[1, l + 1] = ys * inv
-        return (1.0 + k * (1.0 - r), va[l, 0, TOP:TOP + OY, :] + r * yt, va[l, 1, TOP:TOP + OY, :] + r * ys)
-
-    start = (jnp.ones((OY, LN), F32), va[LO - 1, 0, TOP:TOP + OY, :], va[LO - 1, 1, TOP:TOP + OY, :])
-    e, yt, ys = lax.fori_loop(0, LO - 1, up, start)
-    inv = 1.0 / e
-    top_y[0], top_y[1], top_y[2] = yt, ys, inv
+        return 1.0 + k * (1.0 - r), va[l, 0, TOP:TOP + OY, :] + r * yt
+
+    e, yt = lax.fori_loop(0, LO - 1, up, (jnp.ones((OY, LN), F32), va[LO - 1, 0, TOP:TOP + OY, :]))
+    top_y[0], top_y[2] = yt, 1.0 / e
 
     loads[10].wait()
     loads[11].wait()
@@ -540,9 +540,18 @@
     air_r[0] = inv_a
 
     xt0 = (top_y[0] + sea * top_y[3]) * top_y[2]
-    xs0 = (top_y[1] + sea * top_y[4]) * top_y[2]
     lift([sea * xt0, sea])
     send_terms(1)
+
+    lax.fori_loop(0, LO // GROUP, lambda i, carry, f=substep: f(i, carry, tracers=(1,)), 0)
+
+    def up_second(i, ys):
+        l = LO - 2 - i
+        elim_z[1, l + 1] = ys * elim_i[l + 1]
+        return va[l, 1, TOP:TOP + OY, :] + elim_r[l + 1] * ys
+
+    ys = lax.fori_loop(0, LO - 1, up_second, va[LO - 1, 1, TOP:TOP + OY, :])
+    xs0 = (ys + sea * top_y[4]) * top_y[2]
 
     x_out[0] = xt0
     x_out[LO] = xs0
@@ -611,7 +620,7 @@
         V((2 * UNROLL, NF, B, LN), F32), V((256, 256), F32), V((LN, 256), BF16),
         V((ADV, 2, 96, LN), F32), V((ADV, 2, 96, LN), F32), V((ADV, 2, OY, LN), F32), V((ADV, 2, 2, OY, LN), F32),
         V((LO, OY, LN), F32), V((LO, OY, LN), F32), V((LO, OY, LN), F32), V((LO, OY, LN), F32), V((LO, OY, LN), F32),
-        V((LO, OY, LN), F32), V((2, LO, OY, LN), F32), V((5, OY, LN), F32), V((LA, AY, LN), F32), V((LA, AY, LN), F32),
+        V((LO, OY, LN), F32), V((LO, OY, LN), F32), V((2, LO, OY, LN), F32), V((5, OY, LN), F32), V((LA, AY, LN), F32), V((LA, AY, LN), F32),
         V((PL, OY, LN), F32),
         pltpu.SemaphoreType.DMA((13,)), pltpu.SemaphoreType.DMA, pltpu.SemaphoreType.DMA((ADV, 4)),
         pltpu.SemaphoreType.DMA((ADV, 4)), pltpu.SemaphoreType.DMA((3,)), pltpu.SemaphoreType.DMA((3, GX)),

time: 60.1 us -> 59.8 us (level)
  no operation moved by 1% of the time
where the time goes in v5:
time: 59.8 us; the launch traced here: 59.6 us
  Pallas kernels  59 us (99%)
  between operations  0.64 us (1%)
    pallas_call x1, Pallas kernels, shards(): pl.pallas_call(kernel, out_shape=(jax.ShapeDtypeStruct((PL, OY, LN), F32)...  56.6 us
    pallas_call x1, Pallas kernels, shards(): pl.pallas_call(hand_on, out_shape=(jax.ShapeDtypeStruct((PL, OY, LN), F32...  2.35 us

profile of v5, /device:TPU:1, one launch (start us, length us, event | category | flops | bytes accessed | tf_op | source)
XLA Modules:
  0.0 59.6 jit_solution(6568191870777700416)
XLA Ops:
  0.6 56.6 %coupling_step.1 = (f32[60,48,128]{2,1,0:T(8,128)}, f32[16,16,128]{2,1,0:T(8,128)}, f32[4,16,128]{2,1,0:T(8,128)}) custom-call(f32[2,30,48,128]{3,2,1,0:T(8,128)} %tr.1, f32[30,48,128]{2,1,0:T(8,128)} %ue.1, f32[30,48,128]{2,1,0:T(8,128)} %un.1, f32[29,48,128]{2,1,0:T(8,128)} %kap.1, s32[48,128]{1,0:T(8,128)} %land.1, f32[16,16,128]{2,1,0:T(8,128)} %atemp.1, ...), custom_call_target="tpu_custom_call" | custom-call | tf_op jit(solution)/shard_map/coupling_step/pallas_call | solution.py:628
  57.3 2.4 %hand_on.1 = (f32[60,48,128]{2,1,0:T(8,128)}, f32[16,16,128]{2,1,0:T(8,128)}, f32[4,16,128]{2,1,0:T(8,128)}) custom-call(f32[60,48,128]{2,1,0:T(8,128)} %get-tuple-element.9.tr, f32[16,16,128]{2,1,0:T(8,128)} %get-tuple-element.10.air, f32[4,16,128]{2,1,0:T(8,128)} %get-tuple-element.11.sf), custom_call_target="tpu_custom_call" | custom-call | tf_op jit(solution)/shard_map/hand_on/pallas_call | solution.py:645
